TPU v7x, 32 devices: a whole 2x2x4 slice. The times are simulated.
32 devices in a mesh: dp: 8 (over z, x), frame: 4 (over y, core).
Axes of the slice: x: 2, y: 2, z: 4, core: 2. Of those that a mesh axis runs over, the one named last changes fastest.
Arguments:
- features: bfloat16 [8, 16, 32, 64, 128], P('dp', 'frame'), may hold values from -6 to 6
- vis_block: int32 [8, 8, 16, 2], P('dp', None, 'frame'), may hold values from 0 to 31
- vis_count: int32 [8, 8, 16], P('dp', None, 'frame'), may hold values from 1 to 2
- query_frame: int32 [8, 128], P('dp'), may hold values from 0 to 15
- query_block: int32 [8, 128], P('dp'), may hold values from 0 to 31
- query_cell: int32 [8, 128], P('dp'), may hold values from 0 to 63
- cotangent: bfloat16 [8, 4, 128, 16], P('dp', None, 'frame')
- w_in: bfloat16 [128, 384], replicated, may hold values from -0.5 to 0.5
- gain: float32 [384], replicated, may hold values from 0.1 to 1.9
- w_qkv: bfloat16 [384, 1152], replicated, may hold values from -0.3125 to 0.3125
- w_out: bfloat16 [384, 384], replicated, may hold values from -0.3125 to 0.3125
- w_head: bfloat16 [4, 384], replicated, may hold values from -0.3125 to 0.3125
Outputs:
- grad_in: float32 [128, 384], replicated
- grad_gain: float32 [384], replicated
- grad_qkv: float32 [384, 1152], replicated
- grad_out: float32 [384, 384], replicated
- grad_head: float32 [4, 384], replicated
Inputs may be any that keep to these rules, and one draw needn't show every extreme that they name: vis_count counts the leading visible slots of vis_block.
All inputs are finite; a program needn't handle non-finite values.
Results may differ from a plain program's by a relative error of at most 0.012.
Values may be sent and summed in bfloat16 or wider, within the bound.
A program may use at most 64 MiB of HBM per device.

v0:
```python
import jax
import jax.numpy as jnp
from jax import lax
from jax.sharding import PartitionSpec as P

HEADS = 8


def attend(query, keys, values):
    scale = query.shape[-1] ** (-0.5)
    scores = (
        jnp.einsum("nfhd,nghd->nhfg", query.astype(jnp.float32), keys.astype(jnp.float32)) * scale
    )
    probs = jax.nn.softmax(scores, axis=-1).astype(jnp.bfloat16)
    probs = lax.optimization_barrier(probs)
    mixed = jnp.einsum("nhfg,nghd->nfhd", probs.astype(jnp.float32), values.astype(jnp.float32))
    return mixed.astype(jnp.bfloat16)


def inner_rows(left, right):
    return lax.dot_general(
        left, right, (((0,), (0,)), ((), ())), preferred_element_type=jnp.float32
    )


def outer_cols(left, right):
    return lax.dot_general(
        left, right, (((1,), (1,)), ((), ())), preferred_element_type=jnp.float32
    )


def local_grads(corr, cot, w_in, gain, w_qkv, w_out, w_head):
    tracks, frames, width = corr.shape
    total = tracks * frames
    hid = w_in.shape[1]
    head_size = hid // HEADS
    rows = corr.reshape(total, width)
    x_zero = jnp.dot(rows, w_in, preferred_element_type=jnp.float32)
    centred = x_zero - jnp.mean(x_zero, axis=-1, keepdims=True)
    inv_std = lax.rsqrt(jnp.mean(centred * centred, axis=-1, keepdims=True) + 1e-05)
    normed = centred * inv_std
    hidden = (normed * gain).astype(jnp.bfloat16)
    qkv = jnp.dot(hidden, w_qkv, preferred_element_type=jnp.float32).astype(jnp.bfloat16)
    split = qkv.reshape(tracks, frames, 3, HEADS, head_size)
    mixed, backward = jax.vjp(attend, split[:, :, 0], split[:, :, 1], split[:, :, 2])
    mixed = mixed.reshape(total, hid)
    y_out = (x_zero + jnp.dot(mixed, w_out, preferred_element_type=jnp.float32)).astype(
        jnp.bfloat16
    )
    ct_rows = cot.reshape(cot.shape[0], total)
    g_head = jnp.dot(ct_rows, y_out, preferred_element_type=jnp.float32)
    d_y = inner_rows(ct_rows, w_head)
    d_y16 = d_y.astype(jnp.bfloat16)
    g_out = inner_rows(mixed, d_y16)
    d_mixed = outer_cols(d_y16, w_out).astype(jnp.bfloat16)
    d_q, d_k, d_v = backward(d_mixed.reshape(tracks, frames, HEADS, head_size))
    d_qkv = jnp.stack([d_q, d_k, d_v], axis=2).reshape(total, 3 * hid)
    g_qkv = inner_rows(hidden, d_qkv)
    d_hidden = outer_cols(d_qkv, w_qkv)
    g_gain = jnp.sum(d_hidden * normed, axis=0)
    d_norm = d_hidden * gain
    d_x = (
        inv_std
        * (
            d_norm
            - jnp.mean(d_norm, axis=-1, keepdims=True)
            - normed * jnp.mean(d_norm * normed, axis=-1, keepdims=True)
        )
        + d_y
    )
    d_x16 = d_x.astype(jnp.bfloat16)
    g_in = inner_rows(rows, d_x16)
    return (g_in, g_gain, g_qkv, g_out, g_head)


def body(
    features,
    vis_block,
    vis_count,
    query_frame,
    query_block,
    query_cell,
    cotangent,
    w_in,
    gain,
    w_qkv,
    w_out,
    w_head,
):
    feats = features[0]
    fr_dev = feats.shape[0]
    cells = feats.shape[2]
    width = feats.shape[3]
    trk_dev = cotangent.shape[2]
    frame_pos = lax.axis_index("frame")
    frames_q = query_frame[0]
    blocks_q = query_block[0]
    cells_q = query_cell[0]
    local = frames_q - frame_pos * fr_dev
    inside = (local >= 0) & (local < fr_dev)
    picked = feats[jnp.clip(local, 0, fr_dev - 1), blocks_q, cells_q].astype(jnp.float32)
    query = lax.psum_scatter(
        jnp.where(inside[:, None], picked, 0.0).astype(jnp.bfloat16),
        "frame",
        scatter_dimension=0,
        tiled=True,
    )
    groups = vis_block.shape[1]
    slots = vis_block.shape[3]
    frame_ids = jnp.arange(fr_dev, dtype=jnp.int32)[None, :, None]
    patches = feats[frame_ids, vis_block[0]]
    live = jnp.arange(slots, dtype=jnp.int32)[None, None, :] < vis_count[0][:, :, None]
    patches = jnp.where(live[..., None, None], patches, jnp.zeros((), jnp.bfloat16))
    scale = width ** (-0.5)
    outgoing = patches.reshape(groups, fr_dev, slots, cells * width)
    arrived = lax.all_to_all(outgoing, "frame", split_axis=0, concat_axis=1, tiled=True)
    own_groups = arrived.shape[0]
    all_frames = arrived.shape[1]
    arrived = arrived.reshape(own_groups, all_frames, slots, cells, width)
    corr = jnp.einsum(
        "gtc,gfkpc->gtfkp",
        query.reshape(own_groups, -1, width),
        arrived,
        preferred_element_type=jnp.float32,
    )
    corr = (corr * scale).astype(jnp.bfloat16).reshape(trk_dev, all_frames, slots * cells)
    g_in, g_gain, g_qkv, g_out, g_head = local_grads(
        corr, cotangent[0], w_in, gain, w_qkv, w_out, w_head
    )
    s_in, s_gain, s_qkv, s_out, s_head = lax.psum(
        (g_in, g_gain, g_qkv, g_out, g_head), ("dp", "frame")
    )
    return (s_in, s_gain, s_qkv, s_out, s_head)


def solution(mesh):
    in_specs = (
        P("dp", "frame", None, None, None),
        P("dp", None, "frame", None),
        P("dp", None, "frame"),
        P("dp", None),
        P("dp", None),
        P("dp", None),
        P("dp", None, "frame", None),
        P(),
        P(),
        P(),
        P(),
        P(),
    )
    out_specs = (P(), P(), P(), P(), P())
    return jax.shard_map(body, mesh=mesh, in_specs=in_specs, out_specs=out_specs, check_vma=False)
```

profile of v0, /device:TPU:0, one launch (start us, length us, event | category | flops | bytes accessed | tf_op | source)
XLA Modules:
  0.0 243.3 jit_solution(12231735524365807858)
XLA Ops:
  7.2 0.8 fusion.27
  8.0 0.1 copy.30
  8.1 0.1 reshape.207
  8.2 0.5 copy-done
  8.8 1.7 gather_fusion.1
  10.5 1.3 gather.10
  12.0 1.9 broadcast_select_fusion
  14.0 4.2 %all-to-all-start = ((bf16[8,4,2,8192]{3,2,1,0:T(2,128)(2,1)}), bf16[8,4,2,8192]{3,2,1,0:T(2,128)(2,1)}, u32[]{:S(2)}, u32[]{:S(2)}) async-start(bf16[8,4,2,8192]{3,2,1,0:T(2,128)(2,1)} %broadcast_select_fusion), calls=%async_computation.1 | async-start | bytes 2097152 | tf_op jit(solution)/shard_map/all_to_all | solution.py:116
  18.3 1.3 gather_fusion
  19.6 0.7 select_convert_fusion
  20.6 0.3 fusion.44
  20.9 1.6 convolution_convert_fusion.6
  22.5 1.1 copy.42
  23.7 1.9 reshape.197
  25.5 7.9 %all-to-all-done = bf16[8,4,2,8192]{3,2,1,0:T(2,128)(2,1)} async-done(((bf16[8,4,2,8192]{3,2,1,0:T(2,128)(2,1)}), bf16[8,4,2,8192]{3,2,1,0:T(2,128)(2,1)}, u32[]{:S(2)}, u32[]{:S(2)}) %all-to-all-start) | async-done | bytes 1048608 | tf_op jit(solution)/shard_map/all_to_all | solution.py:116
  33.4 3.4 %copy.31 = bf16[2,4,4,2,8192]{4,3,2,1,0:T(2,128)(2,1)} copy(bf16[2,4,4,2,8192]{4,3,2,0,1:T(2,128)(2,1)} %bitcast.12) | data formatting | bytes 2097152 | tf_op jit(solution)/shard_map/all_to_all | solution.py:116
  36.8 1.9 reshape.196
  38.7 5.8 %reduce-scatter.2.cloned.1.call-done = bf16[32,128]{1,0:T(8,128)(2,1)} async-done(((bf16[128,128]{1,0:T(8,128)(2,1)}), bf16[32,128]{1,0:T(8,128)(2,1)}) %reduce-scatter.2.cloned.1.call-update) | async-done | bytes 8208 | tf_op jit(solution)/shard_map/reduce_scatter | solution.py:102
  44.6 1.6 fusion.13
  46.2 0.2 copy.32
  46.4 0.1 reshape_reshape.3
  46.6 0.3 fusion.42
  46.9 0.1 multiply_reduce_fusion.3
  47.1 3.1 %convolution_convert_fusion = bf16[512,1152]{1,0:T(8,128)(2,1)} fusion(bf16[384,1152]{1,0:T(8,128)(2,1)} %param.21, f32[512,384]{0,1:T(8,128)S(1)} %get-tuple-element.19, f32[384]{0:T(512)S(1)} %copy-done.13, f32[512]{0:T(512)S(1)} %add_rsqrt_fusion, f32[512]{0:T(512)S(1)} %broadcast_multiply_fusion.2), kind=kOutput, calls=%fused_computation.4 | convolution fusion | flops 454361088 | bytes 2856448 | tf_op jit(solution)/shard_map/dot_general | solution.py:43
  50.2 5.3 %reshape.198 = bf16[32,16,3,8,48]{4,3,2,1,0:T(8,128)(2,1)} reshape(bf16[512,1152]{1,0:T(8,128)(2,1)} %convolution_convert_fusion) | data formatting | bytes 2359296 | tf_op jit(solution)/shard_map/reshape | solution.py:44
  55.5 3.7 %fusion.41 = (bf16[32,16,1,8,48]{4,3,2,1,0:T(8,128)(2,1)}, bf16[32,16,1,8,48]{4,3,2,1,0:T(8,128)(2,1)}, bf16[32,16,1,8,48]{4,3,2,1,0:T(8,128)(2,1)}) fusion(bf16[32,16,3,8,48]{4,3,2,1,0:T(8,128)(2,1)} %reshape.198), kind=kLoop, calls=%fused_computation.79 | loop fusion | bytes 2359296 | tf_op jit(solution)/shard_map/slice | solution.py:45
  59.1 3.8 %fusion.43 = (f32[32,8,16]{2,1,0:T(8,128)S(1)}, f32[32,8,16,16]{3,2,1,0:T(8,128)}) fusion(bf16[32,16,1,8,48]{4,3,2,1,0:T(8,128)(2,1)} %get-tuple-element.15, bf16[32,16,1,8,48]{4,3,2,1,0:T(8,128)(2,1)} %get-tuple-element.14), kind=kOutput, calls=%fused_computation.81 | convolution fusion | flops 6488079 | bytes 1064960 | tf_op jit(solution)/shard_map/jvp()/sub | solution.py:14
  62.9 2.3 convolution_convert_fusion.5
  65.3 1.9 fusion.5
  67.3 1.9 fusion.7
  69.2 2.5 %fusion.8 = bf16[32,16,1,8,48]{4,1,3,0,2:T(8,128)(2,1)S(1)} fusion(bf16[32,16,1,8,48]{4,3,2,1,0:T(8,128)(2,1)S(1)} %copy-done.8, f32[32,8,16,16]{3,2,1,0:T(8,128)S(1)} %copy-done.7, bf16[32,8,16,16]{3,2,1,0:T(8,128)(2,1)S(1)} %convolution_convert_fusion.5, f32[32,8,16]{2,1,0:T(8,128)S(1)} %neg.6, f32[32,8,16]{2,1,0:T(8,128)S(1)} %get-tuple-element.20), kind=kOutput, calls=%fused_computation.23 | convolution fusion | flops 6815744 | bytes 1212416 | tf_op jit(solution)/shard_map/transpose(jvp(nfhd,nghd->nhfg))/dot_general | solution.py:12
  71.7 1.7 fusion.10
  73.4 0.5 fusion.9
  73.9 0.8 pad_maximum_fusion
  74.7 2.5 %copy.41 = bf16[32,16,3,8,48]{4,3,2,1,0:T(8,128)(2,1)} copy(bf16[32,16,3,8,48]{4,1,3,0,2:T(8,128)(2,1)S(1)} %pad_maximum_fusion) | data formatting | bytes 2359296 | tf_op jit(solution)/shard_map/stack | solution.py:57
  77.1 5.0 %reshape.199 = bf16[512,1152]{1,0:T(8,128)(2,1)} reshape(bf16[32,16,3,8,48]{4,3,2,1,0:T(8,128)(2,1)} %copy.41) | data formatting | bytes 2359296 | tf_op jit(solution)/shard_map/reshape | solution.py:57
  82.1 3.3 %multiply_reduce_fusion.1 = (f32[384]{0:T(512)S(1)}, f32[512]{0:T(512)S(1)}, f32[512]{0:T(512)S(1)}, f32[512,384]{0,1:T(8,128)}) fusion(f32[512,384]{0,1:T(8,128)S(1)} %get-tuple-element.19, f32[512]{0:T(512)S(1)} %add_rsqrt_fusion, f32[512]{0:T(512)S(1)} %broadcast_multiply_fusion.2, f32[384]{0:T(512)S(1)} %copy-done.13, bf16[512,1152]{1,0:T(8,128)(2,1)} %reshape.199, ...), kind=kOutput, calls=%fused_computation.42 | convolution fusion | flops 454556288 | bytes 3648512 | tf_op jit(solution)/shard_map/dot_general | solution.py:27
  85.5 1.9 fusion.38
  87.4 1.2 copy.43
  88.6 2.0 reshape.200
  90.7 2.5 %fusion.22 = f32[384,384]{1,0:T(8,128)} fusion(bf16[512,384]{1,0:T(8,128)(2,1)S(1)} %reshape.200, f32[512,384]{1,0:T(8,128)} %copy-done.1), kind=kOutput, calls=%fused_computation.50 | convolution fusion | flops 151191552 | bytes 1769472 | tf_op jit(solution)/shard_map/dot_general | solution.py:21
  93.2 1.1 fusion.21
  94.3 1.5 fusion.14
  95.8 39.7 %all-reduce = (f32[384]{0:T(512)}, f32[4,384]{1,0:T(4,128)}) all-reduce(f32[384]{0:T(512)S(1)} %get-tuple-element.5, f32[4,384]{1,0:T(4,128)S(1)} %fusion.14), channel_id=1, replica_groups=mesh['dp'=8,'frame'=4] {'dp','frame'}, use_global_device_ids=true, to_apply=%region_10.11 | all-reduce | flops 1920 | bytes 15360 | tf_op jit(solution)/shard_map/psum | solution.py:130
  135.5 95.7 %all-reduce.4.cloned.1.call-done = (f32[128,384]{1,0:T(8,128)}, f32[384,1152]{1,0:T(8,128)}, f32[384,384]{1,0:T(8,128)}) async-done(((f32[128,384]{1,0:T(8,128)}, f32[384,1152]{1,0:T(8,128)}, f32[384,384]{1,0:T(8,128)}), (f32[128,384]{1,0:T(8,128)}, f32[384,1152]{1,0:T(8,128)}, f32[384,384]{1,0:T(8,128)})) %all-reduce.4.cloned.1.call-update) | async-done | bytes 2555920 | tf_op jit(solution)/shard_map/psum | solution.py:130
  231.2 1.7 copy.88
  232.9 2.8 %copy.89 = f32[384,1152]{1,0:T(8,128)} copy(f32[384,1152]{1,0:T(8,128)} %get-tuple-element.27) | data formatting | bytes 3538944
  235.7 0.8 copy.90
  (54 shorter events, 0.6 us)
Async XLA Ops:
  7.2 1.6 copy-start
  8.8 3.0 %copy-start.16 = (s32[1,8,4]{1,2,0:T(4,128)S(1)}, s32[1,8,4]{1,2,0:T(4,128)}, u32[]{:S(2)}) copy-start(s32[1,8,4]{1,2,0:T(4,128)} %param.14) | copy-start | bytes 388
  12.0 6.3 %copy-start.17 = (s32[1,128]{1,0:T(1,128)S(1)}, s32[1,128]{1,0:T(1,128)}, u32[]{:S(2)}) copy-start(s32[1,128]{1,0:T(1,128)} %param.17) | copy-start | bytes 1540
  12.0 6.3 %copy-start.18 = (s32[1,128]{1,0:T(1,128)S(1)}, s32[1,128]{1,0:T(1,128)}, u32[]{:S(2)}) copy-start(s32[1,128]{1,0:T(1,128)} %param.16) | copy-start | bytes 1540
  12.0 6.3 %copy-start.19 = (s32[1,128]{1,0:T(1,128)S(1)}, s32[1,128]{1,0:T(1,128)}, u32[]{:S(2)}) copy-start(s32[1,128]{1,0:T(1,128)} %param.15) | copy-start | bytes 1540
  12.0 8.4 %copy-start.14 = (bf16[1,4,32,16]{2,3,1,0:T(8,128)(2,1)S(1)}, bf16[1,4,32,16]{2,3,1,0:T(8,128)(2,1)}, u32[]{:S(2)}) copy-start(bf16[1,4,32,16]{2,3,1,0:T(8,128)(2,1)} %param.18) | copy-start | bytes 12292
  12.0 8.6 %copy-start.15 = (bf16[4,384]{1,0:T(4,128)(2,1)S(1)}, bf16[4,384]{1,0:T(4,128)(2,1)}, u32[]{:S(2)}) copy-start(bf16[4,384]{1,0:T(4,128)(2,1)} %param.23) | copy-start | bytes 9220
  14.0 19.4 %all-to-all-start = ((bf16[8,4,2,8192]{3,2,1,0:T(2,128)(2,1)}), bf16[8,4,2,8192]{3,2,1,0:T(2,128)(2,1)}, u32[]{:S(2)}, u32[]{:S(2)}) async-start(bf16[8,4,2,8192]{3,2,1,0:T(2,128)(2,1)} %broadcast_select_fusion), calls=%async_computation.1 | async-start | bytes 2097152 | tf_op jit(solution)/shard_map/all_to_all | solution.py:116
  18.2 26.4 %reduce-scatter.2.cloned.1.call-start = ((), (), s32[]{:S(2)}) async-start(), calls=%async_computation.2 | async-start | bytes 40960 | tf_op jit(solution)/shard_map/reduce_scatter | solution.py:102
  20.3 210.9 %all-reduce.4.cloned.1.call-start = ((), (), s32[]{:S(2)}) async-start(), calls=%async_computation.3 | async-start | bytes 5111808 | tf_op jit(solution)/shard_map/psum | solution.py:130
  20.9 4.6 %copy-start.1 = (f32[512,384]{1,0:T(8,128)}, f32[512,384]{1,0:T(8,128)S(1)}, u32[]{:S(2)}) copy-start(f32[512,384]{1,0:T(8,128)S(1)} %fusion.44) | copy-start | bytes 2359300
  36.8 9.7 %copy-start.12 = (bf16[128,384]{1,0:T(8,128)(2,1)S(1)}, bf16[128,384]{1,0:T(8,128)(2,1)}, u32[]{:S(2)}) copy-start(bf16[128,384]{1,0:T(8,128)(2,1)} %param.19) | copy-start | bytes 294916
  38.7 8.3 %copy-start.13 = (f32[384]{0:T(512)S(1)}, f32[384]{0:T(512)}, u32[]{:S(2)}) copy-start(f32[384]{0:T(512)} %param.20) | copy-start | bytes 4612
  62.9 2.4 copy-start.7
  65.3 1.9 copy-start.9
  67.2 1.9 copy-start.8
  69.2 2.5 %copy-start.3 = (bf16[32,16,1,8,48]{4,3,2,1,0:T(8,128)(2,1)S(1)}, bf16[32,16,1,8,48]{4,3,2,1,0:T(8,128)(2,1)}, u32[]{:S(2)}) copy-start(bf16[32,16,1,8,48]{4,3,2,1,0:T(8,128)(2,1)} %get-tuple-element.13) | copy-start | bytes 1179652
  71.7 1.7 copy-start.2
  82.1 3.3 %copy-start.4 = (bf16[512,1152]{1,0:T(8,128)(2,1)S(1)}, bf16[512,1152]{1,0:T(8,128)(2,1)}, u32[]{:S(2)}) copy-start(bf16[512,1152]{1,0:T(8,128)(2,1)} %reshape.199) | copy-start | bytes 3538948
  85.5 1.9 copy-start.5
  90.7 2.5 %copy-start.6 = (f32[512,384]{0,1:T(8,128)S(1)}, f32[512,384]{0,1:T(8,128)}, u32[]{:S(2)}) copy-start(f32[512,384]{0,1:T(8,128)} %copy.42) | copy-start | bytes 2359300
  90.7 2.5 %copy-start.10 = (f32[512,384]{0,1:T(8,128)S(1)}, f32[512,384]{0,1:T(8,128)}, u32[]{:S(2)}) copy-start(f32[512,384]{0,1:T(8,128)} %get-tuple-element.22) | copy-start | bytes 2359300
  231.2 4.5 %copy-start.11 = (f32[384,384]{1,0:T(8,128)S(1)}, f32[384,384]{1,0:T(8,128)}, u32[]{:S(2)}) copy-start(f32[384,384]{1,0:T(8,128)} %get-tuple-element.28) | copy-start | bytes 1769476
Sparse Core Ops, SparseCore 0:
  22.0 22.4 reduce-scatter.1
  94.4 136.7 all-reduce.3
where the time goes:
time: 244 us; the launch traced here: 243 us
  waiting for transfers between devices  109 us (45%)
  blocking collectives  39.7 us (16%)
  local copies, waits for them, and re-layouts  39.1 us (16%)
  matrix products  30 us (12%)
  between operations  14.4 us (6%)
  other arithmetic  6.42 us (3%)
  starting transfers between devices  4.32 us (2%)
    psum x1, waiting for transfers between devices, body(): lax.psum((g_in, g_gain, g_qkv, g_out, g_head), ('dp', 'frame'))  95.7 us
    psum x1, blocking collectives, body(): lax.psum((g_in, g_gain, g_qkv, g_out, g_head), ('dp', 'frame'))  39.7 us
    all_to_all x1, waiting for transfers between devices, body(): lax.all_to_all(outgoing, 'frame', split_axis=0, concat_axis=1, tiled=True)  7.87 us
    unnamed x44, local copies, waits for them, and re-layouts  6.01 us
    reduce_scatter x1, waiting for transfers between devices, body(): lax.psum_scatter(jnp.where(inside[:, None], picked, 0.0).astype(jnp.bfloa...  5.84 us
    dot_general x4, matrix products, inner_rows(): lax.dot_general(left, right, (((0,), (0,)), ((), ())), preferred_element_...  5.82 us
    reshape x1, local copies, waits for them, and re-layouts, local_grads(): split = qkv.reshape(tracks, frames, 3, HEADS, head_size)  5.27 us
    reshape x1, local copies, waits for them, and re-layouts, local_grads(): d_qkv = jnp.stack([d_q, d_k, d_v], axis=2).reshape(total, 3 * hid)  5.01 us
  transfers between devices with their start and end apart: 3, of which 3 were waited for; matrix products, arithmetic and copies ran while one was open for 6% of the time, Pallas kernels for 0%

commit v1 on v0

v1 whole, which is shorter than its diff:
```python
import functools

import jax
import jax.numpy as jnp
from jax import lax
from jax.experimental import pallas as pl
from jax.experimental.pallas import tpu as pltpu
from jax.sharding import PartitionSpec as P

HEADS = 8
LANES = 128
SUB = 8
PACK = 16
MESH = pl.DeviceIdType.MESH
F32 = jnp.float32
BF16 = jnp.bfloat16


def dot_nn(left, right):
    return lax.dot_general(left, right, (((1,), (0,)), ((), ())), preferred_element_type=F32)


def dot_nt(left, right):
    return lax.dot_general(left, right, (((1,), (1,)), ((), ())), preferred_element_type=F32)


def dot_tn(left, right):
    return lax.dot_general(left, right, (((0,), (0,)), ((), ())), preferred_element_type=F32)


def pick_kernel(feats, vis_block, vis_count, q_frame, q_block, q_cell, queries, patches, picked):
    fr_dev, cells, width = feats.shape[1], feats.shape[3], feats.shape[4]
    groups, slots = vis_block.shape[1], vis_block.shape[3]
    tracks = q_frame.shape[1]
    first = lax.axis_index("frame") * fr_dev
    row_id = lax.broadcasted_iota(jnp.int32, (PACK, width), 0)

    @pl.loop(0, tracks // SUB)
    def _(step):
        for i in range(SUB):
            t = step * SUB + i
            local = q_frame[0, t] - first
            cell = q_cell[0, t]
            base = pl.multiple_of(lax.div(cell, PACK) * PACK, PACK)
            inside = jnp.logical_and(local >= 0, local < fr_dev)
            row = jnp.where(inside, lax.rem(cell, PACK), PACK)
            tile = feats[0, jnp.clip(local, 0, fr_dev - 1), q_block[0, t], pl.ds(base, PACK), :]
            kept = jnp.where(row_id == row, tile.astype(F32), 0.0)
            picked[pl.ds(t, 1), :] = jnp.sum(kept, axis=0, keepdims=True)

    queries[...] = picked[...].astype(BF16)
    for g in range(groups):
        for f in range(fr_dev):
            for k in range(slots):
                patch = feats[0, f, vis_block[0, g, f, k]]
                live = k < vis_count[0, g, f]
                patches[g, f, k * cells : (k + 1) * cells] = jnp.where(
                    live, patch, jnp.zeros_like(patch)
                )


def pick(feats, vis_block, vis_count, q_frame, q_block, q_cell):
    fr_dev, cells, width = feats.shape[1], feats.shape[3], feats.shape[4]
    groups, slots = vis_block.shape[1], vis_block.shape[3]
    tracks = q_frame.shape[1]
    smem = pl.BlockSpec(memory_space=pltpu.SMEM)
    vmem = pl.BlockSpec(memory_space=pltpu.VMEM)
    return pl.pallas_call(
        pick_kernel,
        out_shape=[
            jax.ShapeDtypeStruct((tracks, width), BF16),
            jax.ShapeDtypeStruct((groups, fr_dev, slots * cells, width), BF16),
        ],
        in_specs=[vmem] + [smem] * 5,
        out_specs=[vmem, vmem],
        scratch_shapes=[pltpu.VMEM((tracks, width), F32)],
        compiler_params=pltpu.CompilerParams(vmem_limit_bytes=32 * 2**20),
        name="pick",
    )(feats, vis_block, vis_count, q_frame, q_block, q_cell)


def corr_kernel(n, picked, patches, out, q_recv, c_send, q_ssem, q_rsem, c_ssem, c_rsem):
    me = lax.axis_index("frame")
    groups, fr_dev, _, width = patches.shape
    in_group = picked.shape[0] // groups
    own = groups // n
    barrier = pltpu.get_barrier_semaphore()
    for j in range(1, n):
        pl.semaphore_signal(
            barrier, inc=1, device_id={"frame": lax.rem(me + j, n)}, device_id_type=MESH
        )
    pl.semaphore_wait(barrier, n - 1)
    copies = []
    for j in range(1, n):
        copy = pltpu.make_async_remote_copy(
            src_ref=picked,
            dst_ref=q_recv.at[j - 1],
            send_sem=q_ssem.at[j - 1],
            recv_sem=q_rsem.at[j - 1],
            device_id={"frame": lax.rem(me + j, n)},
            device_id_type=MESH,
        )
        copy.start()
        copies.append(copy)
    for copy in copies:
        copy.wait()
    total = picked[...].astype(F32)
    for j in range(1, n):
        total = total + q_recv[j - 1].astype(F32)
    query = total.astype(BF16)

    scale = width ** (-0.5)
    for g in range(groups):
        q_rows = query[g * in_group : (g + 1) * in_group]
        for f in range(fr_dev):
            corr = dot_nt(q_rows, patches[g, f]) * scale
            c_send[g // own, g % own, f] = corr.astype(BF16)
    copies = []
    for j in range(1, n):
        peer = lax.rem(me + j, n)
        copy = pltpu.make_async_remote_copy(
            src_ref=c_send.at[peer],
            dst_ref=out.at[me],
            send_sem=c_ssem.at[j - 1],
            recv_sem=c_rsem.at[j - 1],
            device_id={"frame": peer},
            device_id_type=MESH,
        )
        copy.start()
        copies.append(copy)
    out[me] = c_send[me]
    for copy in copies:
        copy.wait()


def correlate(n, picked, patches):
    groups, fr_dev, cells, _ = patches.shape
    tracks, width = picked.shape
    shape = (n, groups // n, fr_dev, tracks // groups, cells)
    vmem = pl.BlockSpec(memory_space=pltpu.VMEM)
    sems = pltpu.SemaphoreType.DMA((n - 1,))
    return pl.pallas_call(
        functools.partial(corr_kernel, n),
        out_shape=jax.ShapeDtypeStruct(shape, BF16),
        in_specs=[vmem, vmem],
        out_specs=vmem,
        scratch_shapes=[
            pltpu.VMEM((n - 1, tracks, width), BF16),
            pltpu.VMEM(shape, BF16),
            sems,
            sems,
            sems,
            sems,
        ],
        compiler_params=pltpu.CompilerParams(
            collective_id=0, has_side_effects=True, vmem_limit_bytes=32 * 2**20
        ),
        name="correlate",
    )(picked, patches)


def layer_kernel(corr, ct, w_in, gain, w_qkv, w_out, w_head, packed, head_pad, qkv_t, dqkv_t, att_t, datt_t):
    n, own, fr_dev, in_group, width = corr.shape
    frames = n * fr_dev
    hid = w_in.shape[1]
    size = hid // HEADS
    block = frames * SUB
    halves = in_group // SUB
    tokens = own * halves * block

    c32 = corr[...].astype(F32)
    parts = []
    for g in range(own):
        piece = c32[:, g].reshape(frames, halves, SUB, width)
        for half in range(halves):
            parts.append(piece[:, half].reshape(block, width))
    rows32 = jnp.concatenate(parts, axis=0)
    rows = rows32.astype(BF16)
    rows_t = rows32.T.astype(BF16)

    x_zero = dot_nn(w_in[...].T, rows_t)
    centred = x_zero - jnp.mean(x_zero, axis=0, keepdims=True)
    inv_std = lax.rsqrt(jnp.mean(centred * centred, axis=0, keepdims=True) + 1e-05)
    normed = centred * inv_std
    gain_col = gain[...]
    hidden = (normed * gain_col).astype(BF16)
    qkv_t[...] = dot_nn(w_qkv[...].T, hidden).astype(BF16)

    head_pad[...] = jnp.zeros_like(head_pad)
    head_pad[0 : w_head.shape[0], :] = w_head[...].astype(F32)
    ct_rows = ct[...]
    d_y = dot_tn(head_pad[...].astype(BF16), ct_rows)
    d_y16 = d_y.astype(BF16)
    datt_t[...] = dot_nn(w_out[...], d_y16).astype(BF16)

    scale = size ** (-0.5)
    key_id = lax.broadcasted_iota(jnp.int32, (block, block), 0)
    query_id = lax.broadcasted_iota(jnp.int32, (block, block), 1)
    same = lax.rem(key_id, SUB) == lax.rem(query_id, SUB)
    to_exp2 = scale * 1.4426950408889634

    for b in range(tokens // block):
        at = pl.ds(b * block, block)
        for head in range(HEADS):
            mine = pl.ds(head * size, size)
            q = qkv_t[mine, at]
            k = qkv_t[pl.ds(hid + head * size, size), at]
            v = qkv_t[pl.ds(2 * hid + head * size, size), at]
            d_att = datt_t[mine, at]
            scores = jnp.where(same, dot_tn(k, q), -1e30)
            top = jnp.max(scores, axis=0, keepdims=True)
            powers = jnp.exp2((scores - top) * to_exp2)
            probs = powers * (1.0 / jnp.sum(powers, axis=0, keepdims=True))
            probs16 = probs.astype(BF16)
            att_t[mine, at] = dot_nn(v, probs16).astype(BF16)
            d_v = dot_nt(d_att, probs16)
            d_probs = dot_tn(v, d_att).astype(BF16).astype(F32)
            weighted = probs * d_probs
            d_scores = weighted - probs * jnp.sum(weighted, axis=0, keepdims=True)
            d_scores = d_scores.astype(BF16)
            d_q = dot_nn(k, d_scores) * scale
            d_k = dot_nt(q, d_scores) * scale
            dqkv_t[mine, at] = d_q.astype(BF16)
            dqkv_t[pl.ds(hid + head * size, size), at] = d_k.astype(BF16)
            dqkv_t[pl.ds(2 * hid + head * size, size), at] = d_v.astype(BF16)

    def put(row, value):
        for tile in range(value.shape[1] // LANES):
            packed[pl.ds(row, value.shape[0]), :] = value[
                :, tile * LANES : (tile + 1) * LANES
            ].astype(BF16)
            row += value.shape[0]
        return row

    att = att_t[...]
    y_out = (x_zero + dot_nn(w_out[...].T, att)).astype(BF16)
    d_qkv = dqkv_t[...]
    d_hidden = dot_nn(w_qkv[...], d_qkv)
    product = d_hidden * normed
    d_norm = d_hidden * gain_col
    d_x = (
        inv_std
        * (
            d_norm
            - jnp.mean(d_norm, axis=0, keepdims=True)
            - normed * jnp.mean(d_norm * normed, axis=0, keepdims=True)
        )
        + d_y
    )
    row = put(0, dot_nt(rows_t, d_x.astype(BF16)))
    row = put(row, dot_nt(hidden, d_qkv))
    row = put(row, dot_nt(att, d_y16))
    high = product.astype(BF16)
    low = (product - high.astype(F32)).astype(BF16)
    picks = (lax.broadcasted_iota(jnp.int32, (PACK, tokens), 0) == SUB).astype(F32).astype(BF16)
    row = put(row, dot_nt(ct_rows, y_out) + dot_nt(picks, high) + dot_nt(picks, low))
    if row < packed.shape[0]:
        packed[pl.ds(row, packed.shape[0] - row), :] = jnp.zeros(
            (packed.shape[0] - row, LANES), BF16
        )


def packed_rows(shapes, devices):
    rows = sum(-(-r // PACK) * PACK * (c // LANES) for r, c in shapes)
    step = PACK * devices
    return -(-rows // step) * step


def layer(rows, corr, ct, w_in, gain, w_qkv, w_out, w_head):
    hid = w_in.shape[1]
    tokens = ct.shape[1]
    vmem = pl.BlockSpec(memory_space=pltpu.VMEM)
    return pl.pallas_call(
        layer_kernel,
        out_shape=jax.ShapeDtypeStruct((rows, LANES), BF16),
        in_specs=[vmem] * 7,
        out_specs=vmem,
        scratch_shapes=[
            pltpu.VMEM((PACK, hid), F32),
            pltpu.VMEM((3 * hid, tokens), BF16),
            pltpu.VMEM((3 * hid, tokens), BF16),
            pltpu.VMEM((hid, tokens), BF16),
            pltpu.VMEM((hid, tokens), BF16),
        ],
        compiler_params=pltpu.CompilerParams(vmem_limit_bytes=48 * 2**20),
        name="layer",
    )(corr, ct, w_in, gain, w_qkv, w_out, w_head)


def factors(dp, frame):
    core = 2 if frame % 2 == 0 else 1
    mid = frame // core
    low = mid if dp % mid == 0 else 1
    return core, mid, low, dp // low


def stages(dp, frame):
    n_core, n_y, n_x, n_z = factors(dp, frame)
    me_d, me_f = lax.axis_index("dp"), lax.axis_index("frame")
    core, y = lax.rem(me_f, n_core), lax.div(me_f, n_core)
    x, z = lax.rem(me_d, n_x), lax.div(me_d, n_x)
    swap = core if n_core == 2 and n_x == n_y else 0

    def device(core_at, y_at, x_at, z_at):
        return (z_at * n_x + x_at, y_at * n_core + core_at)

    keep = 1 - swap
    return (
        (n_core, core, lambda d: device(d, y, x, z)),
        (n_x, keep * x + swap * y, lambda d: device(core, keep * y + swap * d, keep * d + swap * x, z)),
        (n_y, keep * y + swap * x, lambda d: device(core, keep * d + swap * y, keep * x + swap * d, z)),
        (n_z, z, lambda d: device(core, y, x, d)),
    )


def sum_kernel(dp, frame, given, out, work, r0, r1, r2, r3, *sems):
    plan = stages(dp, frame)
    recvs = (r0, r1, r2, r3)
    barrier = pltpu.get_barrier_semaphore()
    peers = 0
    for size, digit, device in plan:
        for j in range(1, size):
            pl.semaphore_signal(
                barrier, inc=1, device_id=device(lax.rem(digit + j, size)), device_id_type=MESH
            )
            peers += 1
    pl.semaphore_wait(barrier, peers)

    begin, count = 0, given.shape[0]
    for at, (size, digit, device) in enumerate(plan):
        source = given if at == 0 else work
        target = out if at == len(plan) - 1 else work
        part = count // size
        copies = []
        for j in range(1, size):
            peer = lax.rem(digit + j, size)
            copy = pltpu.make_async_remote_copy(
                src_ref=source.at[pl.ds(pl.multiple_of(begin + peer * part, PACK), part)],
                dst_ref=recvs[at].at[j - 1],
                send_sem=sems[4 * at].at[j - 1],
                recv_sem=sems[4 * at + 1].at[j - 1],
                device_id=device(peer),
                device_id_type=MESH,
            )
            copy.start()
            copies.append(copy)
        for copy in copies:
            copy.wait()
        begin = pl.multiple_of(begin + digit * part, PACK)
        count = part
        total = source[pl.ds(begin, part), :].astype(F32)
        for j in range(1, size):
            total = total + recvs[at][j - 1].astype(F32)
        target[pl.ds(begin, part), :] = total.astype(BF16)

    for at in reversed(range(len(plan))):
        size, digit, device = plan[at]
        copies = []
        for j in range(1, size):
            here = out.at[pl.ds(begin, count)]
            copy = pltpu.make_async_remote_copy(
                src_ref=here,
                dst_ref=here,
                send_sem=sems[4 * at + 2].at[j - 1],
                recv_sem=sems[4 * at + 3].at[j - 1],
                device_id=device(lax.rem(digit + j, size)),
                device_id_type=MESH,
            )
            copy.start()
            copies.append(copy)
        for copy in copies:
            copy.wait()
        begin = pl.multiple_of(begin - digit * count, PACK)
        count = count * size


def sum_devices(dp, frame, given):
    rows = given.shape[0]
    vmem = pl.BlockSpec(memory_space=pltpu.VMEM)
    scratch, sems, count = [pltpu.VMEM(given.shape, BF16)], [], rows
    for size in (lambda c, y, x, z: (c, x, y, z))(*factors(dp, frame)):
        count //= size
        slots = max(size - 1, 1)
        scratch.append(pltpu.VMEM((slots, count, LANES), BF16))
        sems += [pltpu.SemaphoreType.DMA((slots,))] * 4
    return pl.pallas_call(
        functools.partial(sum_kernel, dp, frame),
        out_shape=jax.ShapeDtypeStruct(given.shape, BF16),
        in_specs=[vmem],
        out_specs=vmem,
        scratch_shapes=scratch + sems,
        compiler_params=pltpu.CompilerParams(
            collective_id=1, has_side_effects=True, vmem_limit_bytes=32 * 2**20
        ),
        name="sum_devices",
    )(given)


def unpack_kernel(packed, g_in, g_gain, g_qkv, g_out, g_head):
    row = 0
    for ref in (g_in, g_qkv, g_out):
        height = ref.shape[0]
        for tile in range(ref.shape[1] // LANES):
            ref[:, tile * LANES : (tile + 1) * LANES] = packed[pl.ds(row, height), :].astype(F32)
            row += height
    for tile in range(g_head.shape[1] // LANES):
        small = packed[pl.ds(row, PACK), :].astype(F32)
        at = slice(tile * LANES, (tile + 1) * LANES)
        g_head[:, at] = small[0 : g_head.shape[0]]
        g_gain[:, at] = small[SUB : SUB + 1]
        row += PACK


def unpack(packed, shapes):
    vmem = pl.BlockSpec(memory_space=pltpu.VMEM)
    return pl.pallas_call(
        unpack_kernel,
        out_shape=[jax.ShapeDtypeStruct(shape, F32) for shape in shapes],
        in_specs=[vmem],
        out_specs=[vmem] * len(shapes),
        compiler_params=pltpu.CompilerParams(vmem_limit_bytes=32 * 2**20),
        name="unpack",
    )(packed)


def body(
    dp,
    frame,
    features,
    vis_block,
    vis_count,
    query_frame,
    query_block,
    query_cell,
    cotangent,
    w_in,
    gain,
    w_qkv,
    w_out,
    w_head,
):
    outs, trk_dev, frames = cotangent.shape[1:]
    hid = w_in.shape[1]
    ct = cotangent[0].reshape(outs, trk_dev // SUB, SUB, frames)
    ct = jnp.swapaxes(ct, 2, 3).reshape(outs, trk_dev * frames)
    ct = jnp.pad(ct, ((0, PACK - outs), (0, 0)))
    picked, patches = pick(features, vis_block, vis_count, query_frame, query_block, query_cell)
    corr = correlate(frame, picked, patches)
    rows = packed_rows((w_in.shape, w_qkv.shape, w_out.shape, (PACK, hid)), dp * frame)
    packed = layer(rows, corr, ct, w_in, gain.reshape(hid, 1), w_qkv, w_out, w_head)
    summed = sum_devices(dp, frame, packed)
    s_in, s_gain, s_qkv, s_out, s_head = unpack(
        summed, (w_in.shape, (1, hid), w_qkv.shape, w_out.shape, w_head.shape)
    )
    return (s_in, s_gain.reshape(hid), s_qkv, s_out, s_head)


def solution(mesh):
    in_specs = (
        P("dp", "frame", None, None, None),
        P("dp", None, "frame", None),
        P("dp", None, "frame"),
        P("dp", None),
        P("dp", None),
        P("dp", None),
        P("dp", None, "frame", None),
        P(),
        P(),
        P(),
        P(),
        P(),
    )
    out_specs = (P(), P(), P(), P(), P())
    run = functools.partial(body, mesh.shape["dp"], mesh.shape["frame"])
    return jax.shard_map(run, mesh=mesh, in_specs=in_specs, out_specs=out_specs, check_vma=False)
```

time: 244 us -> 73.5 us (0.30)
  waiting for transfers between devices: 109 us -> 0 us
  Pallas kernels: 0 us -> 64.8 us
  blocking collectives: 39.7 us -> 0 us
  local copies, waits for them, and re-layouts: 39.1 us -> 6.98 us
  matrix products: 30 us -> 0 us
  between operations: 14.4 us -> 0.74 us
  other arithmetic: 6.42 us -> 0.6 us
  starting transfers between devices: 4.32 us -> 0 us
    psum x1 -> x0, waiting for transfers between devices: 95.7 us -> none  [body(): lax.psum((g_in, g_gain, g_qkv, g_out, g_head), ('dp', 'frame'))]
    pallas_call x0 -> x5, Pallas kernels: none -> 64.8 us  [the longest x1 39.1 us: sum_devices(): pl.pallas_call(functools.partial(sum_kernel, dp, frame), out_shape=jax.Sh...]
    psum x1 -> x0, blocking collectives: 39.7 us -> none  [body(): lax.psum((g_in, g_gain, g_qkv, g_out, g_head), ('dp', 'frame'))]
    dot_general x15 -> x0, matrix products: 26.2 us -> none  [the longest x4 5.82 us: inner_rows(): lax.dot_general(left, right, (((0,), (0,)), ((), ())), preferred_element_...]
    reshape x5 -> x2, local copies, waits for them, and re-layouts: 16 us -> 0.96 us  [the longest x1 0.83 us: body(): gain.reshape(hid, 1)]
    all_to_all x1 -> x0, waiting for transfers between devices: 7.87 us -> none  [body(): lax.all_to_all(outgoing, 'frame', split_axis=0, concat_axis=1, tiled=True)]
    reduce_scatter x1 -> x0, waiting for transfers between devices: 5.84 us -> none  [body(): lax.psum_scatter(jnp.where(inside[:, None], picked, 0.0).astype(jnp.bfloa...]
    gather x3 -> x0, local copies, waits for them, and re-layouts: 4.29 us -> none  [the longest x2 3.03 us: body(): patches = feats[frame_ids, vis_block[0]]]
  transfers between devices with their start and end apart: 3 -> 0, of which waited for: 3 -> 0; matrix products, arithmetic and copies ran while one was open for 6% -> 0% of each run, Pallas kernels for 0% -> 0%
where the time goes in v1:
time: 73.5 us; the launch traced here: 73.1 us
  Pallas kernels  64.8 us (88%)
  local copies, waits for them, and re-layouts  6.98 us (9%)
  between operations  0.74 us (1%)
    pallas_call x1, Pallas kernels, sum_devices(): pl.pallas_call(functools.partial(sum_kernel, dp, frame), out_shape=jax.Sh...  39.1 us
    pallas_call x1, Pallas kernels, layer(): pl.pallas_call(layer_kernel, out_shape=jax.ShapeDtypeStruct((rows, LANES)...  11.8 us
    pallas_call x1, Pallas kernels, correlate(): pl.pallas_call(functools.partial(corr_kernel, n), out_shape=jax.ShapeDtyp...  9.93 us
    unnamed x19, local copies, waits for them, and re-layouts  5.92 us
    pallas_call x1, Pallas kernels, pick(): pl.pallas_call(pick_kernel, out_shape=[jax.ShapeDtypeStruct((tracks, widt...  2.4 us
    pallas_call x1, Pallas kernels, unpack(): pl.pallas_call(unpack_kernel, out_shape=[jax.ShapeDtypeStruct(shape, F32)...  1.58 us

profile of v1, /device:TPU:0, one launch (start us, length us, event | category | flops | bytes accessed | tf_op | source)
XLA Modules:
  0.0 73.1 jit_solution(12997292470160303341)
XLA Ops:
  0.6 0.8 %copy.21.vis_count = s32[1,8,4]{2,1,0:T(8,128)S(1)} copy(s32[1,8,4]{1,2,0:T(4,128)} %param.14) | data formatting | bytes 256 | tf_op args[2]
  1.4 0.8 %copy.20.vis_block = s32[1,8,4,2]{3,2,1,0:T(4,128)S(1)} copy(s32[1,8,4,2]{1,3,2,0:T(2,128)} %param.13) | data formatting | bytes 512 | tf_op args[1]
  2.2 0.8 %copy.22 = bf16[1,4,32,16]{3,2,1,0:T(8,128)(2,1)S(1)} copy(bf16[1,4,32,16]{2,3,1,0:T(8,128)(2,1)} %param.18) | data formatting | bytes 8192 | tf_op args[6]
  3.0 0.1 copy.23
  3.1 0.1 reshape.19
  3.2 0.0 copy-start.3
  3.2 0.0 copy-start.4
  3.3 0.8 %reshape.22.gain = f32[384,1]{1,0:T(8,128)S(1)} reshape(f32[384]{0:T(512)} %param.20) | data formatting | bytes 3072 | tf_op jit(solution)/shard_map/reshape | solution.py:450
  4.1 0.0 copy-start
  4.1 1.6 %copy-done = bf16[1,4,32,64,128]{4,3,2,1,0:T(8,128)(2,1)S(1)} copy-done((bf16[1,4,32,64,128]{4,3,2,1,0:T(8,128)(2,1)S(1)}, bf16[1,4,32,64,128]{4,3,2,1,0:T(8,128)(2,1)}, u32[]{:S(2)}) %copy-start) | copy-done | bytes 2097176
  5.7 0.0 copy-start.5
  5.7 0.7 copy-done.5
  6.3 0.0 copy-start.6
  6.3 0.7 copy-done.6
  7.0 0.0 copy-start.7
  7.0 0.7 copy-done.7
  7.6 0.0 copy-start.1
  7.7 0.0 copy-start.2
  7.7 2.4 %pick.1 = (bf16[128,128]{1,0:T(8,128)(2,1)S(1)}, bf16[8,4,128,128]{3,2,1,0:T(8,128)(2,1)S(1)}) custom-call(bf16[1,4,32,64,128]{4,3,2,1,0:T(8,128)(2,1)S(1)} %copy-done, s32[1,8,4,2]{3,2,1,0:T(4,128)S(1)} %copy.20.vis_block, s32[1,8,4]{2,1,0:T(8,128)S(1)} %copy.21.vis_count, s32[1,128]{1,0:T(1,128)S(1)} %copy-done.5, s32[1,128]{1,0:T(1,128)S(1)} %copy-done.6, ...), custom_call_target="tpu_custom_call" | custom-call | tf_op jit(solution)/shard_map/pick/pallas_call | solution.py:68
  10.1 9.9 %correlate.1.corr = bf16[4,2,4,16,128]{4,3,2,1,0:T(8,128)(2,1)S(1)} custom-call(bf16[128,128]{1,0:T(8,128)(2,1)S(1)} %get-tuple-element.12.picked, bf16[8,4,128,128]{3,2,1,0:T(8,128)(2,1)S(1)} %get-tuple-element.13.patches), custom_call_target="tpu_custom_call" | custom-call | tf_op jit(solution)/shard_map/correlate/pallas_call | solution.py:142
  20.0 0.0 copy-done.3
  20.0 0.0 copy-done.4
  20.0 0.0 copy-done.1
  20.0 0.0 copy-done.2
  20.0 11.8 %layer.1.given = bf16[5120,128]{1,0:T(8,128)(2,1)S(1)} custom-call(bf16[4,2,4,16,128]{4,3,2,1,0:T(8,128)(2,1)S(1)} %correlate.1.corr, bf16[16,512]{1,0:T(8,128)(2,1)S(1)} %pad.4.ct, bf16[128,384]{1,0:T(8,128)(2,1)S(1)} %copy-done.3, f32[384,1]{1,0:T(8,128)S(1)} %reshape.22.gain, bf16[384,1152]{1,0:T(8,128)(2,1)S(1)} %copy-done.1, ...), custom_call_target="tpu_custom_call" | custom-call | tf_op jit(solution)/shard_map/layer/pallas_call | solution.py:273
  31.9 39.1 %sum_devices.1.packed = bf16[5120,128]{1,0:T(8,128)(2,1)S(1)} custom-call(bf16[5120,128]{1,0:T(8,128)(2,1)S(1)} %layer.1.given), custom_call_target="tpu_custom_call" | custom-call | tf_op jit(solution)/shard_map/sum_devices/pallas_call | solution.py:386
  71.0 1.6 %unpack.1 = (f32[128,384]{1,0:T(8,128)}, f32[1,384]{1,0:T(1,128)S(1)}, f32[384,1152]{1,0:T(8,128)}, f32[384,384]{1,0:T(8,128)}, f32[4,384]{1,0:T(4,128)}) custom-call(bf16[5120,128]{1,0:T(8,128)(2,1)S(1)} %sum_devices.1.packed), custom_call_target="tpu_custom_call" | custom-call | tf_op jit(solution)/shard_map/unpack/pallas_call | solution.py:416
  72.5 0.6 reduce
  (1 shorter events, 0.0 us)
Async XLA Ops:
  3.2 16.8 %copy-start.3 = (bf16[128,384]{1,0:T(8,128)(2,1)S(1)}, bf16[128,384]{1,0:T(8,128)(2,1)}, u32[]{:S(2)}) copy-start(bf16[128,384]{1,0:T(8,128)(2,1)} %w_in.1) | copy-start | bytes 294916
  3.2 16.8 %copy-start.4 = (bf16[4,384]{1,0:T(4,128)(2,1)S(1)}, bf16[4,384]{1,0:T(4,128)(2,1)}, u32[]{:S(2)}) copy-start(bf16[4,384]{1,0:T(4,128)(2,1)} %w_head.1) | copy-start | bytes 9220
  4.1 1.6 %copy-start = (bf16[1,4,32,64,128]{4,3,2,1,0:T(8,128)(2,1)S(1)}, bf16[1,4,32,64,128]{4,3,2,1,0:T(8,128)(2,1)}, u32[]{:S(2)}) copy-start(bf16[1,4,32,64,128]{4,3,2,1,0:T(8,128)(2,1)} %feats.1) | copy-start | bytes 6291460
  5.7 0.7 copy-start.5
  6.3 0.7 copy-start.6
  7.0 0.7 copy-start.7
  7.6 12.4 %copy-start.1 = (bf16[384,1152]{1,0:T(8,128)(2,1)S(1)}, bf16[384,1152]{1,0:T(8,128)(2,1)}, u32[]{:S(2)}) copy-start(bf16[384,1152]{1,0:T(8,128)(2,1)} %w_qkv.1) | copy-start | bytes 2654212
  7.7 12.4 %copy-start.2 = (bf16[384,384]{1,0:T(8,128)(2,1)S(1)}, bf16[384,384]{1,0:T(8,128)(2,1)}, u32[]{:S(2)}) copy-start(bf16[384,384]{1,0:T(8,128)(2,1)} %w_out.1) | copy-start | bytes 884740

commit v2 on v1

--- a/solution.py
+++ b/solution.py
@@ -11,6 +11,7 @@
 LANES = 128
 SUB = 8
 PACK = 16
+CHUNKS = 4
 MESH = pl.DeviceIdType.MESH
 F32 = jnp.float32
 BF16 = jnp.bfloat16
@@ -28,58 +29,131 @@
     return lax.dot_general(left, right, (((0,), (0,)), ((), ())), preferred_element_type=F32)
 
 
-def pick_kernel(feats, vis_block, vis_count, q_frame, q_block, q_cell, queries, patches, picked):
+def pick_kernel(
+    feats, vis_block, vis_count, q_frame, q_block, q_cell, queries, patches,
+    s_block, s_count, s_frame, s_qblock, s_cell, tiles, picked, i_sem, p_sem, q_sem,
+):
     fr_dev, cells, width = feats.shape[1], feats.shape[3], feats.shape[4]
-    groups, slots = vis_block.shape[1], vis_block.shape[3]
+    slots, groups = vis_block.shape[2], vis_block.shape[3]
     tracks = q_frame.shape[1]
     first = lax.axis_index("frame") * fr_dev
-    row_id = lax.broadcasted_iota(jnp.int32, (PACK, width), 0)
+    loads = [
+        pltpu.make_async_copy(src, dst, i_sem.at[i])
+        for i, (src, dst) in enumerate(
+            (
+                (q_frame, s_frame),
+                (q_block, s_qblock),
+                (q_cell, s_cell),
+                (vis_block, s_block),
+                (vis_count, s_count),
+            )
+        )
+    ]
+    for load in loads:
+        load.start()
+    for load in loads[:3]:
+        load.wait()
 
     @pl.loop(0, tracks // SUB)
     def _(step):
         for i in range(SUB):
             t = step * SUB + i
-            local = q_frame[0, t] - first
-            cell = q_cell[0, t]
-            base = pl.multiple_of(lax.div(cell, PACK) * PACK, PACK)
-            inside = jnp.logical_and(local >= 0, local < fr_dev)
-            row = jnp.where(inside, lax.rem(cell, PACK), PACK)
-            tile = feats[0, jnp.clip(local, 0, fr_dev - 1), q_block[0, t], pl.ds(base, PACK), :]
-            kept = jnp.where(row_id == row, tile.astype(F32), 0.0)
-            picked[pl.ds(t, 1), :] = jnp.sum(kept, axis=0, keepdims=True)
-
-    queries[...] = picked[...].astype(BF16)
+            local = jnp.clip(s_frame[0, t] - first, 0, fr_dev - 1)
+            base = pl.multiple_of(lax.div(s_cell[0, t], PACK) * PACK, PACK)
+            pltpu.make_async_copy(
+                feats.at[0, local, s_qblock[0, t], pl.ds(base, PACK), :], tiles.at[t], q_sem
+            ).start()
+
+    for load in loads[3:]:
+        load.wait()
     for g in range(groups):
         for f in range(fr_dev):
             for k in range(slots):
-                patch = feats[0, f, vis_block[0, g, f, k]]
-                live = k < vis_count[0, g, f]
-                patches[g, f, k * cells : (k + 1) * cells] = jnp.where(
-                    live, patch, jnp.zeros_like(patch)
-                )
+                pltpu.make_async_copy(
+                    feats.at[0, f, s_block[0, f, k, g]],
+                    patches.at[g, f, pl.ds(k * cells, cells)],
+                    p_sem,
+                ).start()
+
+    row_id = lax.broadcasted_iota(jnp.int32, (PACK, width), 0)
+    pltpu.make_async_copy(tiles, tiles, q_sem).wait()
+
+    @pl.loop(0, tracks // SUB)
+    def _(step):
+        for i in range(SUB):
+            t = step * SUB + i
+            local = s_frame[0, t] - first
+            inside = jnp.logical_and(local >= 0, local < fr_dev)
+            row = jnp.where(inside, lax.rem(s_cell[0, t], PACK), PACK)
+            kept = jnp.where(row_id == row, tiles[t].astype(F32), 0.0)
+            picked[pl.ds(t, 1), :] = jnp.sum(kept, axis=0, keepdims=True)
+
+    queries[...] = picked[...].astype(BF16)
+    pltpu.make_async_copy(patches, patches, p_sem).wait()
+    for g in range(groups):
+        for f in range(fr_dev):
+            for k in range(slots):
+
+                @pl.when(k >= s_count[0, f, g])
+                def _(g=g, f=f, k=k):
+                    patches[g, f, k * cells : (k + 1) * cells] = jnp.zeros((cells, width), BF16)
 
 
 def pick(feats, vis_block, vis_count, q_frame, q_block, q_cell):
     fr_dev, cells, width = feats.shape[1], feats.shape[3], feats.shape[4]
     groups, slots = vis_block.shape[1], vis_block.shape[3]
     tracks = q_frame.shape[1]
-    smem = pl.BlockSpec(memory_space=pltpu.SMEM)
+    vis_block = jnp.transpose(vis_block, (0, 2, 3, 1))
+    vis_count = jnp.transpose(vis_count, (0, 2, 1))
+    hbm = pl.BlockSpec(memory_space=pltpu.HBM)
     vmem = pl.BlockSpec(memory_space=pltpu.VMEM)
+    arrays = (vis_block, vis_count, q_frame, q_block, q_cell)
     return pl.pallas_call(
         pick_kernel,
         out_shape=[
             jax.ShapeDtypeStruct((tracks, width), BF16),
             jax.ShapeDtypeStruct((groups, fr_dev, slots * cells, width), BF16),
         ],
-        in_specs=[vmem] + [smem] * 5,
+        in_specs=[hbm] * 6,
         out_specs=[vmem, vmem],
-        scratch_shapes=[pltpu.VMEM((tracks, width), F32)],
-        compiler_params=pltpu.CompilerParams(vmem_limit_bytes=32 * 2**20),
+        scratch_shapes=[pltpu.SMEM(array.shape, jnp.int32) for array in arrays]
+        + [
+            pltpu.VMEM((tracks, PACK, width), BF16),
+            pltpu.VMEM((tracks, width), F32),
+            pltpu.SemaphoreType.DMA((5,)),
+            pltpu.SemaphoreType.DMA,
+            pltpu.SemaphoreType.DMA,
+        ],
+        compiler_params=pltpu.CompilerParams(vmem_limit_bytes=60 * 2**20),
         name="pick",
-    )(feats, vis_block, vis_count, q_frame, q_block, q_cell)
-
-
-def corr_kernel(n, picked, patches, out, q_recv, c_send, q_ssem, q_rsem, c_ssem, c_rsem):
+    )(feats, *arrays)
+
+
+def spread_cotangent(cot, tokens):
+    outs, frames, tracks = cot.shape
+    block = frames * SUB
+    token = lax.broadcasted_iota(jnp.int32, (tracks, tokens), 1)
+    track = lax.broadcasted_iota(jnp.int32, (tracks, tokens), 0)
+    wanted = lax.div(token, block) * SUB + lax.rem(token, SUB)
+    choose = jnp.where(track == wanted, 1.0, 0.0).astype(BF16)
+    spread = dot_nn(cot[...].reshape(outs * frames, tracks), choose)
+    token = lax.broadcasted_iota(jnp.int32, (frames, tokens), 1)
+    row = lax.broadcasted_iota(jnp.int32, (frames, tokens), 0)
+    here = lax.div(lax.rem(token, block), SUB) == row
+    return [
+        jnp.sum(
+            jnp.where(here, spread[o * frames : (o + 1) * frames], 0.0), axis=0, keepdims=True
+        )
+        for o in range(outs)
+    ]
+
+
+def corr_kernel(
+    n,
+    picked, patches, cot, gain, w_in, w_qkv, w_out, w_head,
+    out, w_in_t, w_qkv_t, w_out_t, ct, gain_col, d_y, datt_t,
+    q_recv, c_send, head_pad, ct_pad, q_ssem, q_rsem, c_ssem, c_rsem,
+):
     me = lax.axis_index("frame")
     groups, fr_dev, _, width = patches.shape
     in_group = picked.shape[0] // groups
@@ -89,6 +163,8 @@
         pl.semaphore_signal(
             barrier, inc=1, device_id={"frame": lax.rem(me + j, n)}, device_id_type=MESH
         )
+    w_in_t[...] = w_in[...].T
+    w_out_t[...] = w_out[...].T
     pl.semaphore_wait(barrier, n - 1)
     copies = []
     for j in range(1, n):
@@ -102,6 +178,7 @@
         )
         copy.start()
         copies.append(copy)
+    w_qkv_t[...] = w_qkv[...].T
     for copy in copies:
         copy.wait()
     total = picked[...].astype(F32)
@@ -129,24 +206,50 @@
         copy.start()
         copies.append(copy)
     out[me] = c_send[me]
+
+    head_pad[...] = jnp.zeros_like(head_pad)
+    head_pad[0 : w_head.shape[0], :] = w_head[...].astype(F32)
+    ct_pad[...] = jnp.zeros_like(ct_pad)
+    for o, row in enumerate(spread_cotangent(cot, ct_pad.shape[1])):
+        ct_pad[o : o + 1, :] = row
+    ct_rows = ct_pad[...].astype(BF16)
+    ct[...] = ct_rows
+    dy = dot_tn(head_pad[...].astype(BF16), ct_rows)
+    d_y[...] = dy
+    datt_t[...] = dot_nn(w_out[...], dy.astype(BF16)).astype(BF16)
+    gain_col[...] = jnp.broadcast_to(gain[...], (LANES, gain.shape[1])).T[:, 0:1]
     for copy in copies:
         copy.wait()
 
 
-def correlate(n, picked, patches):
+def correlate(n, picked, patches, cot, gain, w_in, w_qkv, w_out, w_head):
     groups, fr_dev, cells, _ = patches.shape
     tracks, width = picked.shape
+    hid = w_in.shape[1]
+    tokens = cot.shape[1] * cot.shape[2]
     shape = (n, groups // n, fr_dev, tracks // groups, cells)
     vmem = pl.BlockSpec(memory_space=pltpu.VMEM)
     sems = pltpu.SemaphoreType.DMA((n - 1,))
+    outs = [
+        (shape, BF16),
+        (w_in.shape[::-1], BF16),
+        (w_qkv.shape[::-1], BF16),
+        (w_out.shape[::-1], BF16),
+        ((PACK, tokens), BF16),
+        ((hid, 1), F32),
+        ((hid, tokens), F32),
+        ((hid, tokens), BF16),
+    ]
     return pl.pallas_call(
         functools.partial(corr_kernel, n),
-        out_shape=jax.ShapeDtypeStruct(shape, BF16),
-        in_specs=[vmem, vmem],
-        out_specs=vmem,
+        out_shape=[jax.ShapeDtypeStruct(*item) for item in outs],
+        in_specs=[vmem] * 8,
+        out_specs=[vmem] * len(outs),
         scratch_shapes=[
             pltpu.VMEM((n - 1, tracks, width), BF16),
             pltpu.VMEM(shape, BF16),
+            pltpu.VMEM((PACK, hid), F32),
+            pltpu.VMEM((PACK, tokens), F32),
             sems,
             sems,
             sems,
@@ -156,13 +259,15 @@
             collective_id=0, has_side_effects=True, vmem_limit_bytes=32 * 2**20
         ),
         name="correlate",
-    )(picked, patches)
-
-
-def layer_kernel(corr, ct, w_in, gain, w_qkv, w_out, w_head, packed, head_pad, qkv_t, dqkv_t, att_t, datt_t):
+    )(picked, patches, cot, gain, w_in, w_qkv, w_out, w_head)
+
+
+def layer_kernel(
+    corr, w_in_t, w_qkv_t, w_out_t, ct, gain, dy_ref, datt_t, w_qkv, packed, qkv_t, dqkv_t, att_t
+):
     n, own, fr_dev, in_group, width = corr.shape
     frames = n * fr_dev
-    hid = w_in.shape[1]
+    hid = w_in_t.shape[0]
     size = hid // HEADS
     block = frames * SUB
     halves = in_group // SUB
@@ -178,20 +283,17 @@
     rows = rows32.astype(BF16)
     rows_t = rows32.T.astype(BF16)
 
-    x_zero = dot_nn(w_in[...].T, rows_t)
+    x_zero = dot_nn(w_in_t[...], rows_t)
     centred = x_zero - jnp.mean(x_zero, axis=0, keepdims=True)
     inv_std = lax.rsqrt(jnp.mean(centred * centred, axis=0, keepdims=True) + 1e-05)
     normed = centred * inv_std
     gain_col = gain[...]
     hidden = (normed * gain_col).astype(BF16)
-    qkv_t[...] = dot_nn(w_qkv[...].T, hidden).astype(BF16)
-
-    head_pad[...] = jnp.zeros_like(head_pad)
-    head_pad[0 : w_head.shape[0], :] = w_head[...].astype(F32)
+    qkv_t[...] = dot_nn(w_qkv_t[...], hidden).astype(BF16)
+
     ct_rows = ct[...]
-    d_y = dot_tn(head_pad[...].astype(BF16), ct_rows)
+    d_y = dy_ref[...]
     d_y16 = d_y.astype(BF16)
-    datt_t[...] = dot_nn(w_out[...], d_y16).astype(BF16)
 
     scale = size ** (-0.5)
     key_id = lax.broadcasted_iota(jnp.int32, (block, block), 0)
@@ -233,7 +335,7 @@
         return row
 
     att = att_t[...]
-    y_out = (x_zero + dot_nn(w_out[...].T, att)).astype(BF16)
+    y_out = (x_zero + dot_nn(w_out_t[...], att)).astype(BF16)
     d_qkv = dqkv_t[...]
     d_hidden = dot_nn(w_qkv[...], d_qkv)
     product = d_hidden * normed
@@ -266,25 +368,22 @@
     return -(-rows // step) * step
 
 
-def layer(rows, corr, ct, w_in, gain, w_qkv, w_out, w_head):
-    hid = w_in.shape[1]
-    tokens = ct.shape[1]
+def layer(rows, prepared, w_qkv):
+    hid, tokens = prepared[-1].shape
     vmem = pl.BlockSpec(memory_space=pltpu.VMEM)
     return pl.pallas_call(
         layer_kernel,
         out_shape=jax.ShapeDtypeStruct((rows, LANES), BF16),
-        in_specs=[vmem] * 7,
+        in_specs=[vmem] * 9,
         out_specs=vmem,
         scratch_shapes=[
-            pltpu.VMEM((PACK, hid), F32),
             pltpu.VMEM((3 * hid, tokens), BF16),
             pltpu.VMEM((3 * hid, tokens), BF16),
-            pltpu.VMEM((hid, tokens), BF16),
             pltpu.VMEM((hid, tokens), BF16),
         ],
         compiler_params=pltpu.CompilerParams(vmem_limit_bytes=48 * 2**20),
         name="layer",
-    )(corr, ct, w_in, gain, w_qkv, w_out, w_head)
+    )(*prepared, w_qkv)
 
 
 def factors(dp, frame):
@@ -313,9 +412,18 @@
     )
 
 
-def sum_kernel(dp, frame, given, out, work, r0, r1, r2, r3, *sems):
+def chunk_bounds(rows, devices):
+    units = rows // (PACK * devices)
+    chunks = min(CHUNKS, units)
+    sizes = [(units + chunks - 1 - c) // chunks * PACK * devices for c in range(chunks)]
+    return [(sum(sizes[:c]), sizes[c]) for c in range(chunks)]
+
+
+def sum_kernel(dp, frame, given, out, work, r0, r1, r2, r3, rs_send, rs_recv, ag_send, ag_recv):
     plan = stages(dp, frame)
+    last = len(plan) - 1
     recvs = (r0, r1, r2, r3)
+    bounds = chunk_bounds(given.shape[0], dp * frame)
     barrier = pltpu.get_barrier_semaphore()
     peers = 0
     for size, digit, device in plan:
@@ -326,69 +434,95 @@
             peers += 1
     pl.semaphore_wait(barrier, peers)
 
-    begin, count = 0, given.shape[0]
-    for at, (size, digit, device) in enumerate(plan):
+    begins = [begin for begin, _ in bounds]
+    counts = [count for _, count in bounds]
+    offsets = [begin for begin, _ in bounds]
+    flying = [[] for _ in bounds]
+
+    def scatter_start(c, at):
+        size, digit, device = plan[at]
         source = given if at == 0 else work
-        target = out if at == len(plan) - 1 else work
-        part = count // size
-        copies = []
+        part = counts[c] // size
+        offsets[c] //= size
         for j in range(1, size):
             peer = lax.rem(digit + j, size)
             copy = pltpu.make_async_remote_copy(
-                src_ref=source.at[pl.ds(pl.multiple_of(begin + peer * part, PACK), part)],
-                dst_ref=recvs[at].at[j - 1],
-                send_sem=sems[4 * at].at[j - 1],
-                recv_sem=sems[4 * at + 1].at[j - 1],
+                src_ref=source.at[pl.ds(pl.multiple_of(begins[c] + peer * part, PACK), part)],
+                dst_ref=recvs[at].at[j - 1, pl.ds(offsets[c], part)],
+                send_sem=rs_send.at[c, at, j - 1],
+                recv_sem=rs_recv.at[c, at, j - 1],
                 device_id=device(peer),
                 device_id_type=MESH,
             )
             copy.start()
-            copies.append(copy)
-        for copy in copies:
+            flying[c].append(copy)
+
+    def scatter_end(c, at):
+        size, digit, device = plan[at]
+        source = given if at == 0 else work
+        target = out if at == last else work
+        part = counts[c] // size
+        for copy in flying[c]:
             copy.wait()
-        begin = pl.multiple_of(begin + digit * part, PACK)
-        count = part
-        total = source[pl.ds(begin, part), :].astype(F32)
+        flying[c] = []
+        begins[c] = pl.multiple_of(begins[c] + digit * part, PACK)
+        counts[c] = part
+        total = source[pl.ds(begins[c], part), :].astype(F32)
         for j in range(1, size):
-            total = total + recvs[at][j - 1].astype(F32)
-        target[pl.ds(begin, part), :] = total.astype(BF16)
-
-    for at in reversed(range(len(plan))):
+            total = total + recvs[at][j - 1, pl.ds(offsets[c], part), :].astype(F32)
+        target[pl.ds(begins[c], part), :] = total.astype(BF16)
+
+    def gather_start(c, at):
         size, digit, device = plan[at]
-        copies = []
         for j in range(1, size):
-            here = out.at[pl.ds(begin, count)]
+            here = out.at[pl.ds(begins[c], counts[c])]
             copy = pltpu.make_async_remote_copy(
                 src_ref=here,
                 dst_ref=here,
-                send_sem=sems[4 * at + 2].at[j - 1],
-                recv_sem=sems[4 * at + 3].at[j - 1],
+                send_sem=ag_send.at[c, at, j - 1],
+                recv_sem=ag_recv.at[c, at, j - 1],
                 device_id=device(lax.rem(digit + j, size)),
                 device_id_type=MESH,
             )
             copy.start()
-            copies.append(copy)
-        for copy in copies:
+            flying[c].append(copy)
+
+    def gather_end(c, at):
+        size, digit, device = plan[at]
+        for copy in flying[c]:
             copy.wait()
-        begin = pl.multiple_of(begin - digit * count, PACK)
-        count = count * size
+        flying[c] = []
+        begins[c] = pl.multiple_of(begins[c] - digit * counts[c], PACK)
+        counts[c] = counts[c] * size
+
+    steps = [(scatter_start, scatter_end, at) for at in range(last + 1)]
+    steps += [(gather_start, gather_end, at) for at in range(last, -1, -1)]
+    for tick in range(len(steps) + len(bounds)):
+        for c in range(len(bounds)):
+            step = tick - c
+            if 1 <= step <= len(steps):
+                steps[step - 1][1](c, steps[step - 1][2])
+            if 0 <= step < len(steps):
+                steps[step][0](c, steps[step][2])
 
 
 def sum_devices(dp, frame, given):
     rows = given.shape[0]
+    n_core, n_y, n_x, n_z = factors(dp, frame)
+    sizes = (n_core, n_x, n_y, n_z)
     vmem = pl.BlockSpec(memory_space=pltpu.VMEM)
-    scratch, sems, count = [pltpu.VMEM(given.shape, BF16)], [], rows
-    for size in (lambda c, y, x, z: (c, x, y, z))(*factors(dp, frame)):
+    scratch, count = [pltpu.VMEM(given.shape, BF16)], rows
+    for size in sizes:
         count //= size
-        slots = max(size - 1, 1)
-        scratch.append(pltpu.VMEM((slots, count, LANES), BF16))
-        sems += [pltpu.SemaphoreType.DMA((slots,))] * 4
+        scratch.append(pltpu.VMEM((max(size - 1, 1), count, LANES), BF16))
+    chunks = len(chunk_bounds(rows, dp * frame))
+    sems = pltpu.SemaphoreType.DMA((chunks, len(sizes), max(max(sizes) - 1, 1)))
     return pl.pallas_call(
         functools.partial(sum_kernel, dp, frame),
         out_shape=jax.ShapeDtypeStruct(given.shape, BF16),
         in_specs=[vmem],
         out_specs=vmem,
-        scratch_shapes=scratch + sems,
+        scratch_shapes=scratch + [sems] * 4,
         compiler_params=pltpu.CompilerParams(
             collective_id=1, has_side_effects=True, vmem_limit_bytes=32 * 2**20
         ),
@@ -407,7 +541,7 @@
         small = packed[pl.ds(row, PACK), :].astype(F32)
         at = slice(tile * LANES, (tile + 1) * LANES)
         g_head[:, at] = small[0 : g_head.shape[0]]
-        g_gain[:, at] = small[SUB : SUB + 1]
+        g_gain[at] = small[SUB]
         row += PACK
 
 
@@ -439,20 +573,16 @@
     w_out,
     w_head,
 ):
-    outs, trk_dev, frames = cotangent.shape[1:]
     hid = w_in.shape[1]
-    ct = cotangent[0].reshape(outs, trk_dev // SUB, SUB, frames)
-    ct = jnp.swapaxes(ct, 2, 3).reshape(outs, trk_dev * frames)
-    ct = jnp.pad(ct, ((0, PACK - outs), (0, 0)))
+    cot = jnp.swapaxes(cotangent[0], 1, 2)
     picked, patches = pick(features, vis_block, vis_count, query_frame, query_block, query_cell)
-    corr = correlate(frame, picked, patches)
+    prepared = correlate(
+        frame, picked, patches, cot, gain.reshape(1, hid), w_in, w_qkv, w_out, w_head
+    )
     rows = packed_rows((w_in.shape, w_qkv.shape, w_out.shape, (PACK, hid)), dp * frame)
-    packed = layer(rows, corr, ct, w_in, gain.reshape(hid, 1), w_qkv, w_out, w_head)
+    packed = layer(rows, prepared, w_qkv)
     summed = sum_devices(dp, frame, packed)
-    s_in, s_gain, s_qkv, s_out, s_head = unpack(
-        summed, (w_in.shape, (1, hid), w_qkv.shape, w_out.shape, w_head.shape)
-    )
-    return (s_in, s_gain.reshape(hid), s_qkv, s_out, s_head)
+    return tuple(unpack(summed, (w_in.shape, gain.shape, w_qkv.shape, w_out.shape, w_head.shape)))
 
 
 def solution(mesh):

time: 73.5 us -> 71.8 us (0.977)
  local copies, waits for them, and re-layouts: 6.98 us -> 2.78 us
  Pallas kernels: 64.8 us -> 68 us
    unnamed x19 -> x14, local copies, waits for them, and re-layouts: 5.92 us -> 2 us
    pallas_call x1, Pallas kernels: 2.4 us -> 4.61 us  [pick(): pl.pallas_call(pick_kernel, out_shape=[jax.ShapeDtypeStruct((tracks, widt...]
    pallas_call x1, Pallas kernels: 39.1 us -> 40.6 us  [sum_devices(): pl.pallas_call(functools.partial(sum_kernel, dp, frame), out_shape=jax.Sh...]
where the time goes in v2:
time: 71.8 us; the launch traced here: 71.5 us
  Pallas kernels  68 us (95%)
  local copies, waits for them, and re-layouts  2.78 us (4%)
  between operations  0.75 us (1%)
    pallas_call x1, Pallas kernels, sum_devices(): pl.pallas_call(functools.partial(sum_kernel, dp, frame), out_shape=jax.Sh...  40.6 us
    pallas_call x1, Pallas kernels, layer(): pl.pallas_call(layer_kernel, out_shape=jax.ShapeDtypeStruct((rows, LANES)...  11.3 us
    pallas_call x1, Pallas kernels, correlate(): pl.pallas_call(functools.partial(corr_kernel, n), out_shape=[jax.ShapeDty...  9.89 us
    pallas_call x1, Pallas kernels, pick(): pl.pallas_call(pick_kernel, out_shape=[jax.ShapeDtypeStruct((tracks, widt...  4.61 us
    unnamed x14, local copies, waits for them, and re-layouts  2 us
    pallas_call x1, Pallas kernels, unpack(): pl.pallas_call(unpack_kernel, out_shape=[jax.ShapeDtypeStruct(shape, F32)...  1.58 us

profile of v2, /device:TPU:0, one launch (start us, length us, event | category | flops | bytes accessed | tf_op | source)
XLA Modules:
  0.0 71.5 jit_solution(11852658604087535910)
XLA Ops:
  0.6 0.0 copy-start
  0.6 0.0 copy-start.6
  0.7 0.0 copy-start.2
  0.7 0.0 copy-start.3
  0.7 0.0 copy-start.5
  0.7 0.8 %reshape.13.gain = f32[1,384]{1,0:T(1,128)S(1)} reshape(f32[384]{0:T(512)} %param.20) | data formatting | bytes 3072 | tf_op jit(solution)/shard_map/reshape | solution.py:580
  1.5 4.6 %pick.1 = (bf16[128,128]{1,0:T(8,128)(2,1)}, bf16[8,4,128,128]{3,2,1,0:T(8,128)(2,1)}) custom-call(bf16[1,4,32,64,128]{4,3,2,1,0:T(8,128)(2,1)} %feats.1, s32[1,4,2,8]{3,2,1,0:T(2,128)} %bitcast.6, s32[1,4,8]{2,1,0:T(4,128)} %bitcast.7, s32[1,128]{1,0:T(1,128)} %q_frame.1, s32[1,128]{1,0:T(1,128)} %q_block.1, s32[1,128]{1,0:T(1,128)} %q_cell.1), custom_call_target="tpu_custom_call" | custom-call | tf_op jit(solution)/shard_map/pick/pallas_call | solution.py:111
  6.1 0.0 copy-done
  6.1 0.0 copy-done.6
  6.1 0.0 copy-done.2
  6.1 0.0 copy-done.3
  6.1 0.0 copy-done.5
  6.1 0.0 copy-start.1
  6.1 1.2 %copy-done.1 = bf16[8,4,128,128]{3,2,1,0:T(8,128)(2,1)S(1)} copy-done((bf16[8,4,128,128]{3,2,1,0:T(8,128)(2,1)S(1)}, bf16[8,4,128,128]{3,2,1,0:T(8,128)(2,1)}, u32[]{:S(2)}) %copy-start.1) | copy-done | bytes 1048600
  7.4 0.0 copy-start.4
  7.4 0.8 %copy-done.4 = bf16[128,128]{1,0:T(8,128)(2,1)S(1)} copy-done((bf16[128,128]{1,0:T(8,128)(2,1)S(1)}, bf16[128,128]{1,0:T(8,128)(2,1)}, u32[]{:S(2)}) %copy-start.4) | copy-done | bytes 32792
  8.1 9.9 %correlate.1 = (bf16[4,2,4,16,128]{4,3,2,1,0:T(8,128)(2,1)S(1)}, bf16[384,128]{1,0:T(8,128)(2,1)S(1)}, bf16[1152,384]{1,0:T(8,128)(2,1)S(1)}, bf16[384,384]{1,0:...) custom-call(bf16[128,128]{1,0:T(8,128)(2,1)S(1)} %copy-done.4, ...), custom_call_target="tpu_custom_call" | custom-call | tf_op jit(solution)/shard_map/correlate/pallas_call | solution.py:243
  18.0 11.3 %layer.1.given = bf16[5120,128]{1,0:T(8,128)(2,1)S(1)} custom-call(bf16[4,2,4,16,128]{4,3,2,1,0:T(8,128)(2,1)S(1)} %get-tuple-element.17.corr, bf16[384,128]{1,0:T(8,128)(2,1)S(1)} %get-tuple-element.18.w_in_t, bf16[1152,384]{1,0:T(8,128)(2,1)S(1)} %get-tuple-element.19.w_qkv_t, bf16[384,384]{1,0:T(8,128)(2,1)S(1)} %get-tuple-element.20.w_out_t, ...), custom_call_target="tpu_custom_call" | custom-call | tf_op jit(solution)/shard_map/layer/pallas_call | solution.py:374
  29.3 40.6 %sum_devices.1.packed = bf16[5120,128]{1,0:T(8,128)(2,1)S(1)} custom-call(bf16[5120,128]{1,0:T(8,128)(2,1)S(1)} %layer.1.given), custom_call_target="tpu_custom_call" | custom-call | tf_op jit(solution)/shard_map/sum_devices/pallas_call | solution.py:520
  69.9 1.6 %unpack.1 = (f32[128,384]{1,0:T(8,128)}, f32[384]{0:T(512)}, f32[384,1152]{1,0:T(8,128)}, f32[384,384]{1,0:T(8,128)}, f32[4,384]{1,0:T(4,128)}) custom-call(bf16[5120,128]{1,0:T(8,128)(2,1)S(1)} %sum_devices.1.packed), custom_call_target="tpu_custom_call" | custom-call | tf_op jit(solution)/shard_map/unpack/pallas_call | solution.py:550
Async XLA Ops:
  0.6 5.4 %copy-start = (bf16[384,1152]{1,0:T(8,128)(2,1)S(1)}, bf16[384,1152]{1,0:T(8,128)(2,1)}, u32[]{:S(2)}) copy-start(bf16[384,1152]{1,0:T(8,128)(2,1)} %w_qkv.3) | copy-start | bytes 2654212
  0.6 5.4 %copy-start.6 = (bf16[4,384]{1,0:T(4,128)(2,1)S(1)}, bf16[4,384]{1,0:T(4,128)(2,1)}, u32[]{:S(2)}) copy-start(bf16[4,384]{1,0:T(4,128)(2,1)} %w_head.1) | copy-start | bytes 9220
  0.7 5.4 %copy-start.2 = (bf16[384,384]{1,0:T(8,128)(2,1)S(1)}, bf16[384,384]{1,0:T(8,128)(2,1)}, u32[]{:S(2)}) copy-start(bf16[384,384]{1,0:T(8,128)(2,1)} %w_out.1) | copy-start | bytes 884740
  0.7 5.4 %copy-start.3 = (bf16[128,384]{1,0:T(8,128)(2,1)S(1)}, bf16[128,384]{1,0:T(8,128)(2,1)}, u32[]{:S(2)}) copy-start(bf16[128,384]{1,0:T(8,128)(2,1)} %w_in.1) | copy-start | bytes 294916
  0.7 5.4 %copy-start.5 = (bf16[1,4,32,16]{2,3,1,0:T(8,128)(2,1)S(1)}, bf16[1,4,32,16]{2,3,1,0:T(8,128)(2,1)}, u32[]{:S(2)}) copy-start(bf16[1,4,32,16]{2,3,1,0:T(8,128)(2,1)} %param.18) | copy-start | bytes 12292
  6.1 1.2 %copy-start.1 = (bf16[8,4,128,128]{3,2,1,0:T(8,128)(2,1)S(1)}, bf16[8,4,128,128]{3,2,1,0:T(8,128)(2,1)}, u32[]{:S(2)}) copy-start(bf16[8,4,128,128]{3,2,1,0:T(8,128)(2,1)} %get-tuple-element.16.patches) | copy-start | bytes 3145732
  7.4 0.8 %copy-start.4 = (bf16[128,128]{1,0:T(8,128)(2,1)S(1)}, bf16[128,128]{1,0:T(8,128)(2,1)}, u32[]{:S(2)}) copy-start(bf16[128,128]{1,0:T(8,128)(2,1)} %get-tuple-element.15.picked) | copy-start | bytes 98308

commit v3 on v2

--- a/solution.py
+++ b/solution.py
@@ -11,7 +11,7 @@
 LANES = 128
 SUB = 8
 PACK = 16
-CHUNKS = 4
+CHUNKS = 3
 MESH = pl.DeviceIdType.MESH
 F32 = jnp.float32
 BF16 = jnp.bfloat16
@@ -403,11 +403,9 @@
     def device(core_at, y_at, x_at, z_at):
         return (z_at * n_x + x_at, y_at * n_core + core_at)
 
-    keep = 1 - swap
     return (
         (n_core, core, lambda d: device(d, y, x, z)),
-        (n_x, keep * x + swap * y, lambda d: device(core, keep * y + swap * d, keep * d + swap * x, z)),
-        (n_y, keep * y + swap * x, lambda d: device(core, keep * d + swap * y, keep * x + swap * d, z)),
+        (n_x * n_y, y * n_x + x, lambda d: device(core, lax.div(d, n_x), lax.rem(d, n_x), z)),
         (n_z, z, lambda d: device(core, y, x, d)),
     )
 
@@ -419,10 +417,10 @@
     return [(sum(sizes[:c]), sizes[c]) for c in range(chunks)]
 
 
-def sum_kernel(dp, frame, given, out, work, r0, r1, r2, r3, rs_send, rs_recv, ag_send, ag_recv):
+def sum_kernel(dp, frame, given, out, work, r0, r1, r2, rs_send, rs_recv, ag_send, ag_recv):
     plan = stages(dp, frame)
     last = len(plan) - 1
-    recvs = (r0, r1, r2, r3)
+    recvs = (r0, r1, r2)
     bounds = chunk_bounds(given.shape[0], dp * frame)
     barrier = pltpu.get_barrier_semaphore()
     peers = 0
@@ -497,19 +495,18 @@
 
     steps = [(scatter_start, scatter_end, at) for at in range(last + 1)]
     steps += [(gather_start, gather_end, at) for at in range(last, -1, -1)]
-    for tick in range(len(steps) + len(bounds)):
+    for step in range(len(steps) + 1):
         for c in range(len(bounds)):
-            step = tick - c
-            if 1 <= step <= len(steps):
+            if step > 0:
                 steps[step - 1][1](c, steps[step - 1][2])
-            if 0 <= step < len(steps):
+            if step < len(steps):
                 steps[step][0](c, steps[step][2])
 
 
 def sum_devices(dp, frame, given):
     rows = given.shape[0]
     n_core, n_y, n_x, n_z = factors(dp, frame)
-    sizes = (n_core, n_x, n_y, n_z)
+    sizes = (n_core, n_x * n_y, n_z)
     vmem = pl.BlockSpec(memory_space=pltpu.VMEM)
     scratch, count = [pltpu.VMEM(given.shape, BF16)], rows
     for size in sizes:

time: 71.8 us -> 59.8 us (0.83)
  Pallas kernels: 68 us -> 55.9 us
    pallas_call x1, Pallas kernels: 40.6 us -> 28.5 us  [sum_devices(): pl.pallas_call(functools.partial(sum_kernel, dp, frame), out_shape=jax.Sh...]
where the time goes in v3:
time: 59.8 us; the launch traced here: 59.4 us
  Pallas kernels  55.9 us (93%)
  local copies, waits for them, and re-layouts  2.78 us (5%)
  between operations  0.75 us (1%)
    pallas_call x1, Pallas kernels, sum_devices(): pl.pallas_call(functools.partial(sum_kernel, dp, frame), out_shape=jax.Sh...  28.5 us
    pallas_call x1, Pallas kernels, layer(): pl.pallas_call(layer_kernel, out_shape=jax.ShapeDtypeStruct((rows, LANES)...  11.3 us
    pallas_call x1, Pallas kernels, correlate(): pl.pallas_call(functools.partial(corr_kernel, n), out_shape=[jax.ShapeDty...  9.88 us
    pallas_call x1, Pallas kernels, pick(): pl.pallas_call(pick_kernel, out_shape=[jax.ShapeDtypeStruct((tracks, widt...  4.61 us
    unnamed x14, local copies, waits for them, and re-layouts  2 us
    pallas_call x1, Pallas kernels, unpack(): pl.pallas_call(unpack_kernel, out_shape=[jax.ShapeDtypeStruct(shape, F32)...  1.58 us

profile of v3, /device:TPU:0, one launch (start us, length us, event | category | flops | bytes accessed | tf_op | source)
XLA Modules:
  0.0 59.4 jit_solution(2558397852254302434)
XLA Ops:
  0.6 0.0 copy-start
  0.6 0.0 copy-start.6
  0.7 0.0 copy-start.2
  0.7 0.0 copy-start.3
  0.7 0.0 copy-start.5
  0.7 0.8 %reshape.13.gain = f32[1,384]{1,0:T(1,128)S(1)} reshape(f32[384]{0:T(512)} %param.20) | data formatting | bytes 3072 | tf_op jit(solution)/shard_map/reshape | solution.py:577
  1.5 4.6 %pick.1 = (bf16[128,128]{1,0:T(8,128)(2,1)}, bf16[8,4,128,128]{3,2,1,0:T(8,128)(2,1)}) custom-call(bf16[1,4,32,64,128]{4,3,2,1,0:T(8,128)(2,1)} %feats.1, s32[1,4,2,8]{3,2,1,0:T(2,128)} %bitcast.6, s32[1,4,8]{2,1,0:T(4,128)} %bitcast.7, s32[1,128]{1,0:T(1,128)} %q_frame.1, s32[1,128]{1,0:T(1,128)} %q_block.1, s32[1,128]{1,0:T(1,128)} %q_cell.1), custom_call_target="tpu_custom_call" | custom-call | tf_op jit(solution)/shard_map/pick/pallas_call | solution.py:111
  6.1 0.0 copy-done
  6.1 0.0 copy-done.6
  6.1 0.0 copy-done.2
  6.1 0.0 copy-done.3
  6.1 0.0 copy-done.5
  6.1 0.0 copy-start.1
  6.1 1.2 %copy-done.1 = bf16[8,4,128,128]{3,2,1,0:T(8,128)(2,1)S(1)} copy-done((bf16[8,4,128,128]{3,2,1,0:T(8,128)(2,1)S(1)}, bf16[8,4,128,128]{3,2,1,0:T(8,128)(2,1)}, u32[]{:S(2)}) %copy-start.1) | copy-done | bytes 1048600
  7.4 0.0 copy-start.4
  7.4 0.8 %copy-done.4 = bf16[128,128]{1,0:T(8,128)(2,1)S(1)} copy-done((bf16[128,128]{1,0:T(8,128)(2,1)S(1)}, bf16[128,128]{1,0:T(8,128)(2,1)}, u32[]{:S(2)}) %copy-start.4) | copy-done | bytes 32792
  8.1 9.9 %correlate.1 = (bf16[4,2,4,16,128]{4,3,2,1,0:T(8,128)(2,1)S(1)}, bf16[384,128]{1,0:T(8,128)(2,1)S(1)}, bf16[1152,384]{1,0:T(8,128)(2,1)S(1)}, bf16[384,384]{1,0:...) custom-call(bf16[128,128]{1,0:T(8,128)(2,1)S(1)} %copy-done.4, ...), custom_call_target="tpu_custom_call" | custom-call | tf_op jit(solution)/shard_map/correlate/pallas_call | solution.py:243
  18.0 11.3 %layer.1.given = bf16[5120,128]{1,0:T(8,128)(2,1)S(1)} custom-call(bf16[4,2,4,16,128]{4,3,2,1,0:T(8,128)(2,1)S(1)} %get-tuple-element.17.corr, bf16[384,128]{1,0:T(8,128)(2,1)S(1)} %get-tuple-element.18.w_in_t, bf16[1152,384]{1,0:T(8,128)(2,1)S(1)} %get-tuple-element.19.w_qkv_t, bf16[384,384]{1,0:T(8,128)(2,1)S(1)} %get-tuple-element.20.w_out_t, ...), custom_call_target="tpu_custom_call" | custom-call | tf_op jit(solution)/shard_map/layer/pallas_call | solution.py:374
  29.3 28.5 %sum_devices.1.packed = bf16[5120,128]{1,0:T(8,128)(2,1)S(1)} custom-call(bf16[5120,128]{1,0:T(8,128)(2,1)S(1)} %layer.1.given), custom_call_target="tpu_custom_call" | custom-call | tf_op jit(solution)/shard_map/sum_devices/pallas_call | solution.py:517
  57.9 1.6 %unpack.1 = (f32[128,384]{1,0:T(8,128)}, f32[384]{0:T(512)}, f32[384,1152]{1,0:T(8,128)}, f32[384,384]{1,0:T(8,128)}, f32[4,384]{1,0:T(4,128)}) custom-call(bf16[5120,128]{1,0:T(8,128)(2,1)S(1)} %sum_devices.1.packed), custom_call_target="tpu_custom_call" | custom-call | tf_op jit(solution)/shard_map/unpack/pallas_call | solution.py:547
Async XLA Ops:
  0.6 5.4 %copy-start = (bf16[384,1152]{1,0:T(8,128)(2,1)S(1)}, bf16[384,1152]{1,0:T(8,128)(2,1)}, u32[]{:S(2)}) copy-start(bf16[384,1152]{1,0:T(8,128)(2,1)} %w_qkv.3) | copy-start | bytes 2654212
  0.6 5.4 %copy-start.6 = (bf16[4,384]{1,0:T(4,128)(2,1)S(1)}, bf16[4,384]{1,0:T(4,128)(2,1)}, u32[]{:S(2)}) copy-start(bf16[4,384]{1,0:T(4,128)(2,1)} %w_head.1) | copy-start | bytes 9220
  0.7 5.4 %copy-start.2 = (bf16[384,384]{1,0:T(8,128)(2,1)S(1)}, bf16[384,384]{1,0:T(8,128)(2,1)}, u32[]{:S(2)}) copy-start(bf16[384,384]{1,0:T(8,128)(2,1)} %w_out.1) | copy-start | bytes 884740
  0.7 5.4 %copy-start.3 = (bf16[128,384]{1,0:T(8,128)(2,1)S(1)}, bf16[128,384]{1,0:T(8,128)(2,1)}, u32[]{:S(2)}) copy-start(bf16[128,384]{1,0:T(8,128)(2,1)} %w_in.1) | copy-start | bytes 294916
  0.7 5.4 %copy-start.5 = (bf16[1,4,32,16]{2,3,1,0:T(8,128)(2,1)S(1)}, bf16[1,4,32,16]{2,3,1,0:T(8,128)(2,1)}, u32[]{:S(2)}) copy-start(bf16[1,4,32,16]{2,3,1,0:T(8,128)(2,1)} %param.18) | copy-start | bytes 12292
  6.1 1.2 %copy-start.1 = (bf16[8,4,128,128]{3,2,1,0:T(8,128)(2,1)S(1)}, bf16[8,4,128,128]{3,2,1,0:T(8,128)(2,1)}, u32[]{:S(2)}) copy-start(bf16[8,4,128,128]{3,2,1,0:T(8,128)(2,1)} %get-tuple-element.16.patches) | copy-start | bytes 3145732
  7.4 0.8 %copy-start.4 = (bf16[128,128]{1,0:T(8,128)(2,1)S(1)}, bf16[128,128]{1,0:T(8,128)(2,1)}, u32[]{:S(2)}) copy-start(bf16[128,128]{1,0:T(8,128)(2,1)} %get-tuple-element.15.picked) | copy-start | bytes 98308

commit v4 on v3

--- a/solution.py
+++ b/solution.py
@@ -148,8 +148,8 @@
     ]
 
 
-def corr_kernel(
-    n,
+def exchange(
+    n, plan,
     picked, patches, cot, gain, w_in, w_qkv, w_out, w_head,
     out, w_in_t, w_qkv_t, w_out_t, ct, gain_col, d_y, datt_t,
     q_recv, c_send, head_pad, ct_pad, q_ssem, q_rsem, c_ssem, c_rsem,
@@ -159,13 +159,14 @@
     in_group = picked.shape[0] // groups
     own = groups // n
     barrier = pltpu.get_barrier_semaphore()
-    for j in range(1, n):
-        pl.semaphore_signal(
-            barrier, inc=1, device_id={"frame": lax.rem(me + j, n)}, device_id_type=MESH
-        )
+    greeted = [{"frame": lax.rem(me + j, n)} for j in range(1, n)]
+    for size, digit, device in plan:
+        greeted += [device(lax.rem(digit + j, size)) for j in range(1, size)]
+    for peer in greeted:
+        pl.semaphore_signal(barrier, inc=1, device_id=peer, device_id_type=MESH)
     w_in_t[...] = w_in[...].T
     w_out_t[...] = w_out[...].T
-    pl.semaphore_wait(barrier, n - 1)
+    pl.semaphore_wait(barrier, len(greeted))
     copies = []
     for j in range(1, n):
         copy = pltpu.make_async_remote_copy(
@@ -222,48 +223,8 @@
         copy.wait()
 
 
-def correlate(n, picked, patches, cot, gain, w_in, w_qkv, w_out, w_head):
-    groups, fr_dev, cells, _ = patches.shape
-    tracks, width = picked.shape
-    hid = w_in.shape[1]
-    tokens = cot.shape[1] * cot.shape[2]
-    shape = (n, groups // n, fr_dev, tracks // groups, cells)
-    vmem = pl.BlockSpec(memory_space=pltpu.VMEM)
-    sems = pltpu.SemaphoreType.DMA((n - 1,))
-    outs = [
-        (shape, BF16),
-        (w_in.shape[::-1], BF16),
-        (w_qkv.shape[::-1], BF16),
-        (w_out.shape[::-1], BF16),
-        ((PACK, tokens), BF16),
-        ((hid, 1), F32),
-        ((hid, tokens), F32),
-        ((hid, tokens), BF16),
-    ]
-    return pl.pallas_call(
-        functools.partial(corr_kernel, n),
-        out_shape=[jax.ShapeDtypeStruct(*item) for item in outs],
-        in_specs=[vmem] * 8,
-        out_specs=[vmem] * len(outs),
-        scratch_shapes=[
-            pltpu.VMEM((n - 1, tracks, width), BF16),
-            pltpu.VMEM(shape, BF16),
-            pltpu.VMEM((PACK, hid), F32),
-            pltpu.VMEM((PACK, tokens), F32),
-            sems,
-            sems,
-            sems,
-            sems,
-        ],
-        compiler_params=pltpu.CompilerParams(
-            collective_id=0, has_side_effects=True, vmem_limit_bytes=32 * 2**20
-        ),
-        name="correlate",
-    )(picked, patches, cot, gain, w_in, w_qkv, w_out, w_head)
-
-
-def layer_kernel(
-    corr, w_in_t, w_qkv_t, w_out_t, ct, gain, dy_ref, datt_t, w_qkv, packed, qkv_t, dqkv_t, att_t
+def layer(
+    corr, w_in_t, w_qkv_t, w_out_t, ct, gain, dy_ref, datt_t, w_qkv, packed, qkv_t, dqkv_t, att_t, ready
 ):
     n, own, fr_dev, in_group, width = corr.shape
     frames = n * fr_dev
@@ -332,12 +293,17 @@
                 :, tile * LANES : (tile + 1) * LANES
             ].astype(BF16)
             row += value.shape[0]
+        ready(row)
         return row
 
+    row = 0
     att = att_t[...]
+    for tile in range(hid // LANES):
+        row = put(row, dot_nt(att, d_y16[tile * LANES : (tile + 1) * LANES]))
+    for tile in range(3 * hid // LANES):
+        row = put(row, dot_nt(hidden, dqkv_t[tile * LANES : (tile + 1) * LANES, :]))
     y_out = (x_zero + dot_nn(w_out_t[...], att)).astype(BF16)
-    d_qkv = dqkv_t[...]
-    d_hidden = dot_nn(w_qkv[...], d_qkv)
+    d_hidden = dot_nn(w_qkv[...], dqkv_t[...])
     product = d_hidden * normed
     d_norm = d_hidden * gain_col
     d_x = (
@@ -349,9 +315,7 @@
         )
         + d_y
     )
-    row = put(0, dot_nt(rows_t, d_x.astype(BF16)))
-    row = put(row, dot_nt(hidden, d_qkv))
-    row = put(row, dot_nt(att, d_y16))
+    row = put(row, dot_nt(rows_t, d_x.astype(BF16)))
     high = product.astype(BF16)
     low = (product - high.astype(F32)).astype(BF16)
     picks = (lax.broadcasted_iota(jnp.int32, (PACK, tokens), 0) == SUB).astype(F32).astype(BF16)
@@ -360,30 +324,13 @@
         packed[pl.ds(row, packed.shape[0] - row), :] = jnp.zeros(
             (packed.shape[0] - row, LANES), BF16
         )
+    ready(packed.shape[0])
 
 
 def packed_rows(shapes, devices):
     rows = sum(-(-r // PACK) * PACK * (c // LANES) for r, c in shapes)
     step = PACK * devices
     return -(-rows // step) * step
-
-
-def layer(rows, prepared, w_qkv):
-    hid, tokens = prepared[-1].shape
-    vmem = pl.BlockSpec(memory_space=pltpu.VMEM)
-    return pl.pallas_call(
-        layer_kernel,
-        out_shape=jax.ShapeDtypeStruct((rows, LANES), BF16),
-        in_specs=[vmem] * 9,
-        out_specs=vmem,
-        scratch_shapes=[
-            pltpu.VMEM((3 * hid, tokens), BF16),
-            pltpu.VMEM((3 * hid, tokens), BF16),
-            pltpu.VMEM((hid, tokens), BF16),
-        ],
-        compiler_params=pltpu.CompilerParams(vmem_limit_bytes=48 * 2**20),
-        name="layer",
-    )(*prepared, w_qkv)
 
 
 def factors(dp, frame):
@@ -417,21 +364,8 @@
     return [(sum(sizes[:c]), sizes[c]) for c in range(chunks)]
 
 
-def sum_kernel(dp, frame, given, out, work, r0, r1, r2, rs_send, rs_recv, ag_send, ag_recv):
-    plan = stages(dp, frame)
+def device_sum(plan, bounds, given, out, work, recvs, rs_send, rs_recv, ag_send, ag_recv):
     last = len(plan) - 1
-    recvs = (r0, r1, r2)
-    bounds = chunk_bounds(given.shape[0], dp * frame)
-    barrier = pltpu.get_barrier_semaphore()
-    peers = 0
-    for size, digit, device in plan:
-        for j in range(1, size):
-            pl.semaphore_signal(
-                barrier, inc=1, device_id=device(lax.rem(digit + j, size)), device_id_type=MESH
-            )
-            peers += 1
-    pl.semaphore_wait(barrier, peers)
-
     begins = [begin for begin, _ in bounds]
     counts = [count for _, count in bounds]
     offsets = [begin for begin, _ in bounds]
@@ -495,41 +429,106 @@
 
     steps = [(scatter_start, scatter_end, at) for at in range(last + 1)]
     steps += [(gather_start, gather_end, at) for at in range(last, -1, -1)]
-    for step in range(len(steps) + 1):
-        for c in range(len(bounds)):
-            if step > 0:
+    started = []
+
+    def ready(row):
+        for c, (begin, count) in enumerate(bounds):
+            if begin + count <= row and c not in started:
+                started.append(c)
+                scatter_start(c, 0)
+
+    def finish():
+        for step in range(1, len(steps) + 1):
+            for c in range(len(bounds)):
                 steps[step - 1][1](c, steps[step - 1][2])
-            if step < len(steps):
-                steps[step][0](c, steps[step][2])
-
-
-def sum_devices(dp, frame, given):
-    rows = given.shape[0]
+                if step < len(steps):
+                    steps[step][0](c, steps[step][2])
+
+    return ready, finish
+
+
+def train_kernel(
+    dp, frame,
+    picked, patches, cot, gain, w_in, w_qkv, w_out, w_head,
+    summed,
+    corr, w_in_t, w_qkv_t, w_out_t, ct, gain_col, d_y, datt_t,
+    q_recv, c_send, head_pad, ct_pad, q_ssem, q_rsem, c_ssem, c_rsem,
+    qkv_t, dqkv_t, att_t,
+    given, work, r0, r1, r2, rs_send, rs_recv, ag_send, ag_recv,
+):
+    plan = stages(dp, frame)
+    bounds = chunk_bounds(given.shape[0], dp * frame)
+    exchange(
+        frame, plan, picked, patches, cot, gain, w_in, w_qkv, w_out, w_head,
+        corr, w_in_t, w_qkv_t, w_out_t, ct, gain_col, d_y, datt_t,
+        q_recv, c_send, head_pad, ct_pad, q_ssem, q_rsem, c_ssem, c_rsem,
+    )
+    ready, finish = device_sum(
+        plan, bounds, given, summed, work, (r0, r1, r2), rs_send, rs_recv, ag_send, ag_recv
+    )
+    layer(
+        corr, w_in_t, w_qkv_t, w_out_t, ct, gain_col, d_y, datt_t, w_qkv,
+        given, qkv_t, dqkv_t, att_t, ready,
+    )
+    finish()
+
+
+def train(dp, frame, rows, picked, patches, cot, gain, w_in, w_qkv, w_out, w_head):
+    groups, fr_dev, cells, _ = patches.shape
+    tracks, width = picked.shape
+    hid = w_in.shape[1]
+    tokens = cot.shape[1] * cot.shape[2]
+    shape = (frame, groups // frame, fr_dev, tracks // groups, cells)
+    vmem = pl.BlockSpec(memory_space=pltpu.VMEM)
+    peers = pltpu.SemaphoreType.DMA((frame - 1,))
+    scratch = [
+        pltpu.VMEM(*item)
+        for item in (
+            (shape, BF16),
+            (w_in.shape[::-1], BF16),
+            (w_qkv.shape[::-1], BF16),
+            (w_out.shape[::-1], BF16),
+            ((PACK, tokens), BF16),
+            ((hid, 1), F32),
+            ((hid, tokens), F32),
+            ((hid, tokens), BF16),
+            ((frame - 1, tracks, width), BF16),
+            (shape, BF16),
+            ((PACK, hid), F32),
+            ((PACK, tokens), F32),
+        )
+    ]
+    scratch += [peers] * 4
+    scratch += [
+        pltpu.VMEM((3 * hid, tokens), BF16),
+        pltpu.VMEM((3 * hid, tokens), BF16),
+        pltpu.VMEM((hid, tokens), BF16),
+    ]
     n_core, n_y, n_x, n_z = factors(dp, frame)
     sizes = (n_core, n_x * n_y, n_z)
-    vmem = pl.BlockSpec(memory_space=pltpu.VMEM)
-    scratch, count = [pltpu.VMEM(given.shape, BF16)], rows
+    scratch += [pltpu.VMEM((rows, LANES), BF16)] * 2
+    count = rows
     for size in sizes:
         count //= size
         scratch.append(pltpu.VMEM((max(size - 1, 1), count, LANES), BF16))
     chunks = len(chunk_bounds(rows, dp * frame))
-    sems = pltpu.SemaphoreType.DMA((chunks, len(sizes), max(max(sizes) - 1, 1)))
+    scratch += [pltpu.SemaphoreType.DMA((chunks, len(sizes), max(max(sizes) - 1, 1)))] * 4
     return pl.pallas_call(
-        functools.partial(sum_kernel, dp, frame),
-        out_shape=jax.ShapeDtypeStruct(given.shape, BF16),
-        in_specs=[vmem],
+        functools.partial(train_kernel, dp, frame),
+        out_shape=jax.ShapeDtypeStruct((rows, LANES), BF16),
+        in_specs=[vmem] * 8,
         out_specs=vmem,
-        scratch_shapes=scratch + [sems] * 4,
+        scratch_shapes=scratch,
         compiler_params=pltpu.CompilerParams(
-            collective_id=1, has_side_effects=True, vmem_limit_bytes=32 * 2**20
+            collective_id=0, has_side_effects=True, vmem_limit_bytes=48 * 2**20
         ),
-        name="sum_devices",
-    )(given)
+        name="train",
+    )(picked, patches, cot, gain, w_in, w_qkv, w_out, w_head)
 
 
 def unpack_kernel(packed, g_in, g_gain, g_qkv, g_out, g_head):
     row = 0
-    for ref in (g_in, g_qkv, g_out):
+    for ref in (g_out, g_qkv, g_in):
         height = ref.shape[0]
         for tile in range(ref.shape[1] // LANES):
             ref[:, tile * LANES : (tile + 1) * LANES] = packed[pl.ds(row, height), :].astype(F32)
@@ -573,12 +572,10 @@
     hid = w_in.shape[1]
     cot = jnp.swapaxes(cotangent[0], 1, 2)
     picked, patches = pick(features, vis_block, vis_count, query_frame, query_block, query_cell)
-    prepared = correlate(
-        frame, picked, patches, cot, gain.reshape(1, hid), w_in, w_qkv, w_out, w_head
-    )
     rows = packed_rows((w_in.shape, w_qkv.shape, w_out.shape, (PACK, hid)), dp * frame)
-    packed = layer(rows, prepared, w_qkv)
-    summed = sum_devices(dp, frame, packed)
+    summed = train(
+        dp, frame, rows, picked, patches, cot, gain.reshape(1, hid), w_in, w_qkv, w_out, w_head
+    )
     return tuple(unpack(summed, (w_in.shape, gain.shape, w_qkv.shape, w_out.shape, w_head.shape)))
 
 

time: 59.8 us -> 57.9 us (0.968)
  Pallas kernels: 55.9 us -> 54.1 us
    pallas_call x3 -> x1, Pallas kernels: 49.7 us -> 47.9 us  [train(): pl.pallas_call(functools.partial(train_kernel, dp, frame), out_shape=jax....]
where the time goes in v4:
time: 57.9 us; the launch traced here: 57.6 us
  Pallas kernels  54.1 us (93%)
  local copies, waits for them, and re-layouts  2.78 us (5%)
  between operations  0.74 us (1%)
    pallas_call x1, Pallas kernels, train(): pl.pallas_call(functools.partial(train_kernel, dp, frame), out_shape=jax....  47.9 us
    pallas_call x1, Pallas kernels, pick(): pl.pallas_call(pick_kernel, out_shape=[jax.ShapeDtypeStruct((tracks, widt...  4.6 us
    unnamed x14, local copies, waits for them, and re-layouts  2 us
    pallas_call x1, Pallas kernels, unpack(): pl.pallas_call(unpack_kernel, out_shape=[jax.ShapeDtypeStruct(shape, F32)...  1.57 us

profile of v4, /device:TPU:0, one launch (start us, length us, event | category | flops | bytes accessed | tf_op | source)
XLA Modules:
  0.0 57.6 jit_solution(10450032108771742368)
XLA Ops:
  0.6 0.0 copy-start.6
  0.6 0.0 copy-start.2
  0.7 0.0 copy-start.1
  0.7 0.0 copy-start.3
  0.7 0.0 copy-start.5
  0.7 0.8 %reshape.13.gain = f32[1,384]{1,0:T(1,128)S(1)} reshape(f32[384]{0:T(512)} %param.20) | data formatting | bytes 3072 | tf_op jit(solution)/shard_map/reshape | solution.py:577
  1.5 4.6 %pick.1 = (bf16[128,128]{1,0:T(8,128)(2,1)}, bf16[8,4,128,128]{3,2,1,0:T(8,128)(2,1)}) custom-call(bf16[1,4,32,64,128]{4,3,2,1,0:T(8,128)(2,1)} %feats.1, s32[1,4,2,8]{3,2,1,0:T(2,128)} %bitcast.6, s32[1,4,8]{2,1,0:T(4,128)} %bitcast.7, s32[1,128]{1,0:T(1,128)} %q_frame.1, s32[1,128]{1,0:T(1,128)} %q_block.1, s32[1,128]{1,0:T(1,128)} %q_cell.1), custom_call_target="tpu_custom_call" | custom-call | tf_op jit(solution)/shard_map/pick/pallas_call | solution.py:111
  6.1 0.0 copy-done.6
  6.1 0.0 copy-done.2
  6.1 0.0 copy-done.1
  6.1 0.0 copy-done.3
  6.1 0.0 copy-done.5
  6.1 0.0 copy-start
  6.1 1.2 %copy-done = bf16[8,4,128,128]{3,2,1,0:T(8,128)(2,1)S(1)} copy-done((bf16[8,4,128,128]{3,2,1,0:T(8,128)(2,1)S(1)}, bf16[8,4,128,128]{3,2,1,0:T(8,128)(2,1)}, u32[]{:S(2)}) %copy-start) | copy-done | bytes 1048600
  7.4 0.0 copy-start.4
  7.4 0.8 %copy-done.4 = bf16[128,128]{1,0:T(8,128)(2,1)S(1)} copy-done((bf16[128,128]{1,0:T(8,128)(2,1)S(1)}, bf16[128,128]{1,0:T(8,128)(2,1)}, u32[]{:S(2)}) %copy-start.4) | copy-done | bytes 32792
  8.1 47.9 %train.1.packed = bf16[5120,128]{1,0:T(8,128)(2,1)S(1)} custom-call(bf16[128,128]{1,0:T(8,128)(2,1)S(1)} %copy-done.4, bf16[8,4,128,128]{3,2,1,0:T(8,128)(2,1)S(1)} %copy-done, bf16[4,16,32]{2,1,0:T(8,128)(2,1)S(1)} %bitcast.5, f32[1,384]{1,0:T(1,128)S(1)} %reshape.13.gain, bf16[128,384]{1,0:T(8,128)(2,1)S(1)} %copy-done.3, bf16[384,1152]{1,0:T(8,128)(2,1)S(1)} %copy-done.1, ...), custom_call_target="tpu_custom_call" | custom-call | tf_op jit(solution)/shard_map/train/pallas_call | solution.py:516
  56.1 1.6 %unpack.1 = (f32[128,384]{1,0:T(8,128)}, f32[384]{0:T(512)}, f32[384,1152]{1,0:T(8,128)}, f32[384,384]{1,0:T(8,128)}, f32[4,384]{1,0:T(4,128)}) custom-call(bf16[5120,128]{1,0:T(8,128)(2,1)S(1)} %train.1.packed), custom_call_target="tpu_custom_call" | custom-call | tf_op jit(solution)/shard_map/unpack/pallas_call | solution.py:546
Async XLA Ops:
  0.6 5.4 %copy-start.6 = (bf16[4,384]{1,0:T(4,128)(2,1)S(1)}, bf16[4,384]{1,0:T(4,128)(2,1)}, u32[]{:S(2)}) copy-start(bf16[4,384]{1,0:T(4,128)(2,1)} %w_head.1) | copy-start | bytes 9220
  0.6 5.4 %copy-start.2 = (bf16[384,384]{1,0:T(8,128)(2,1)S(1)}, bf16[384,384]{1,0:T(8,128)(2,1)}, u32[]{:S(2)}) copy-start(bf16[384,384]{1,0:T(8,128)(2,1)} %w_out.1) | copy-start | bytes 884740
  0.7 5.4 %copy-start.1 = (bf16[384,1152]{1,0:T(8,128)(2,1)S(1)}, bf16[384,1152]{1,0:T(8,128)(2,1)}, u32[]{:S(2)}) copy-start(bf16[384,1152]{1,0:T(8,128)(2,1)} %w_qkv.1) | copy-start | bytes 2654212
  0.7 5.4 %copy-start.3 = (bf16[128,384]{1,0:T(8,128)(2,1)S(1)}, bf16[128,384]{1,0:T(8,128)(2,1)}, u32[]{:S(2)}) copy-start(bf16[128,384]{1,0:T(8,128)(2,1)} %w_in.1) | copy-start | bytes 294916
  0.7 5.4 %copy-start.5 = (bf16[1,4,32,16]{2,3,1,0:T(8,128)(2,1)S(1)}, bf16[1,4,32,16]{2,3,1,0:T(8,128)(2,1)}, u32[]{:S(2)}) copy-start(bf16[1,4,32,16]{2,3,1,0:T(8,128)(2,1)} %param.18) | copy-start | bytes 12292
  6.1 1.2 %copy-start = (bf16[8,4,128,128]{3,2,1,0:T(8,128)(2,1)S(1)}, bf16[8,4,128,128]{3,2,1,0:T(8,128)(2,1)}, u32[]{:S(2)}) copy-start(bf16[8,4,128,128]{3,2,1,0:T(8,128)(2,1)} %get-tuple-element.8.patches) | copy-start | bytes 3145732
  7.4 0.8 %copy-start.4 = (bf16[128,128]{1,0:T(8,128)(2,1)S(1)}, bf16[128,128]{1,0:T(8,128)(2,1)}, u32[]{:S(2)}) copy-start(bf16[128,128]{1,0:T(8,128)(2,1)} %get-tuple-element.7.picked) | copy-start | bytes 98308

commit v5 on v4

--- a/solution.py
+++ b/solution.py
@@ -12,6 +12,7 @@
 SUB = 8
 PACK = 16
 CHUNKS = 3
+LOOP = 32
 MESH = pl.DeviceIdType.MESH
 F32 = jnp.float32
 BF16 = jnp.bfloat16
@@ -78,10 +79,10 @@
     row_id = lax.broadcasted_iota(jnp.int32, (PACK, width), 0)
     pltpu.make_async_copy(tiles, tiles, q_sem).wait()
 
-    @pl.loop(0, tracks // SUB)
+    @pl.loop(0, tracks // LOOP)
     def _(step):
-        for i in range(SUB):
-            t = step * SUB + i
+        for i in range(LOOP):
+            t = step * LOOP + i
             local = s_frame[0, t] - first
             inside = jnp.logical_and(local >= 0, local < fr_dev)
             row = jnp.where(inside, lax.rem(s_cell[0, t], PACK), PACK)
@@ -218,7 +219,7 @@
     dy = dot_tn(head_pad[...].astype(BF16), ct_rows)
     d_y[...] = dy
     datt_t[...] = dot_nn(w_out[...], dy.astype(BF16)).astype(BF16)
-    gain_col[...] = jnp.broadcast_to(gain[...], (LANES, gain.shape[1])).T[:, 0:1]
+    gain_col[...] = jnp.broadcast_to(gain[...].reshape(1, -1), (LANES, gain.shape[0])).T[:, 0:1]
     for copy in copies:
         copy.wait()
 
@@ -574,7 +575,7 @@
     picked, patches = pick(features, vis_block, vis_count, query_frame, query_block, query_cell)
     rows = packed_rows((w_in.shape, w_qkv.shape, w_out.shape, (PACK, hid)), dp * frame)
     summed = train(
-        dp, frame, rows, picked, patches, cot, gain.reshape(1, hid), w_in, w_qkv, w_out, w_head
+        dp, frame, rows, picked, patches, cot, gain, w_in, w_qkv, w_out, w_head
     )
     return tuple(unpack(summed, (w_in.shape, gain.shape, w_qkv.shape, w_out.shape, w_head.shape)))
 

time: 57.9 us -> 57.2 us (0.988)
  local copies, waits for them, and re-layouts: 2.78 us -> 2 us
    reshape x1 -> x0, local copies, waits for them, and re-layouts: 0.78 us -> none  [body(): gain.reshape(1, hid)]
    unnamed x14 -> x16, local copies, waits for them, and re-layouts: 2 us -> 2 us
where the time goes in v5:
time: 57.2 us; the launch traced here: 56.8 us
  Pallas kernels  54.1 us (95%)
  local copies, waits for them, and re-layouts  2 us (3%)
  between operations  0.76 us (1%)
    pallas_call x1, Pallas kernels, train(): pl.pallas_call(functools.partial(train_kernel, dp, frame), out_shape=jax....  47.9 us
    pallas_call x1, Pallas kernels, pick(): pl.pallas_call(pick_kernel, out_shape=[jax.ShapeDtypeStruct((tracks, widt...  4.61 us
    unnamed x16, local copies, waits for them, and re-layouts  2 us
    pallas_call x1, Pallas kernels, unpack(): pl.pallas_call(unpack_kernel, out_shape=[jax.ShapeDtypeStruct(shape, F32)...  1.57 us

profile of v5, /device:TPU:0, one launch (start us, length us, event | category | flops | bytes accessed | tf_op | source)
XLA Modules:
  0.0 56.8 jit_solution(14032262157395384860)
XLA Ops:
  0.6 0.0 copy-start.6
  0.6 0.0 copy-start.2
  0.7 0.0 copy-start.1
  0.7 0.0 copy-start.7
  0.7 0.0 copy-start.3
  0.7 0.0 copy-start.5
  0.7 4.6 %pick.1 = (bf16[128,128]{1,0:T(8,128)(2,1)}, bf16[8,4,128,128]{3,2,1,0:T(8,128)(2,1)}) custom-call(bf16[1,4,32,64,128]{4,3,2,1,0:T(8,128)(2,1)} %feats.1, s32[1,4,2,8]{3,2,1,0:T(2,128)} %bitcast.6, s32[1,4,8]{2,1,0:T(4,128)} %bitcast.7, s32[1,128]{1,0:T(1,128)} %q_frame.1, s32[1,128]{1,0:T(1,128)} %q_block.1, s32[1,128]{1,0:T(1,128)} %q_cell.1), custom_call_target="tpu_custom_call" | custom-call | tf_op jit(solution)/shard_map/pick/pallas_call | solution.py:112
  5.3 0.0 copy-done.6
  5.3 0.0 copy-done.2
  5.3 0.0 copy-done.1
  5.3 0.0 copy-done.7
  5.4 0.0 copy-done.3
  5.4 0.0 copy-done.5
  5.4 0.0 copy-start
  5.4 1.2 %copy-done = bf16[8,4,128,128]{3,2,1,0:T(8,128)(2,1)S(1)} copy-done((bf16[8,4,128,128]{3,2,1,0:T(8,128)(2,1)S(1)}, bf16[8,4,128,128]{3,2,1,0:T(8,128)(2,1)}, u32[]{:S(2)}) %copy-start) | copy-done | bytes 1048600
  6.6 0.0 copy-start.4
  6.6 0.8 %copy-done.4 = bf16[128,128]{1,0:T(8,128)(2,1)S(1)} copy-done((bf16[128,128]{1,0:T(8,128)(2,1)S(1)}, bf16[128,128]{1,0:T(8,128)(2,1)}, u32[]{:S(2)}) %copy-start.4) | copy-done | bytes 32792
  7.4 47.9 %train.1.packed = bf16[5120,128]{1,0:T(8,128)(2,1)S(1)} custom-call(bf16[128,128]{1,0:T(8,128)(2,1)S(1)} %copy-done.4, bf16[8,4,128,128]{3,2,1,0:T(8,128)(2,1)S(1)} %copy-done, bf16[4,16,32]{2,1,0:T(8,128)(2,1)S(1)} %bitcast.5, f32[384]{0:T(512)S(1)} %copy-done.7, bf16[128,384]{1,0:T(8,128)(2,1)S(1)} %copy-done.3, bf16[384,1152]{1,0:T(8,128)(2,1)S(1)} %copy-done.1, ...), custom_call_target="tpu_custom_call" | custom-call | tf_op jit(solution)/shard_map/train/pallas_call | solution.py:517
  55.3 1.6 %unpack.1 = (f32[128,384]{1,0:T(8,128)}, f32[384]{0:T(512)}, f32[384,1152]{1,0:T(8,128)}, f32[384,384]{1,0:T(8,128)}, f32[4,384]{1,0:T(4,128)}) custom-call(bf16[5120,128]{1,0:T(8,128)(2,1)S(1)} %train.1.packed), custom_call_target="tpu_custom_call" | custom-call | tf_op jit(solution)/shard_map/unpack/pallas_call | solution.py:547
Async XLA Ops:
  0.6 4.7 %copy-start.6 = (bf16[4,384]{1,0:T(4,128)(2,1)S(1)}, bf16[4,384]{1,0:T(4,128)(2,1)}, u32[]{:S(2)}) copy-start(bf16[4,384]{1,0:T(4,128)(2,1)} %w_head.1) | copy-start | bytes 9220
  0.6 4.7 %copy-start.2 = (bf16[384,384]{1,0:T(8,128)(2,1)S(1)}, bf16[384,384]{1,0:T(8,128)(2,1)}, u32[]{:S(2)}) copy-start(bf16[384,384]{1,0:T(8,128)(2,1)} %w_out.1) | copy-start | bytes 884740
  0.7 4.7 %copy-start.1 = (bf16[384,1152]{1,0:T(8,128)(2,1)S(1)}, bf16[384,1152]{1,0:T(8,128)(2,1)}, u32[]{:S(2)}) copy-start(bf16[384,1152]{1,0:T(8,128)(2,1)} %w_qkv.1) | copy-start | bytes 2654212
  0.7 4.7 %copy-start.7 = (f32[384]{0:T(512)S(1)}, f32[384]{0:T(512)}, u32[]{:S(2)}) copy-start(f32[384]{0:T(512)} %gain.1) | copy-start | bytes 4612
  0.7 4.7 %copy-start.3 = (bf16[128,384]{1,0:T(8,128)(2,1)S(1)}, bf16[128,384]{1,0:T(8,128)(2,1)}, u32[]{:S(2)}) copy-start(bf16[128,384]{1,0:T(8,128)(2,1)} %w_in.1) | copy-start | bytes 294916
  0.7 4.7 %copy-start.5 = (bf16[1,4,32,16]{2,3,1,0:T(8,128)(2,1)S(1)}, bf16[1,4,32,16]{2,3,1,0:T(8,128)(2,1)}, u32[]{:S(2)}) copy-start(bf16[1,4,32,16]{2,3,1,0:T(8,128)(2,1)} %param.18) | copy-start | bytes 12292
  5.4 1.2 %copy-start = (bf16[8,4,128,128]{3,2,1,0:T(8,128)(2,1)S(1)}, bf16[8,4,128,128]{3,2,1,0:T(8,128)(2,1)}, u32[]{:S(2)}) copy-start(bf16[8,4,128,128]{3,2,1,0:T(8,128)(2,1)} %get-tuple-element.8.patches) | copy-start | bytes 3145732
  6.6 0.8 %copy-start.4 = (bf16[128,128]{1,0:T(8,128)(2,1)S(1)}, bf16[128,128]{1,0:T(8,128)(2,1)}, u32[]{:S(2)}) copy-start(bf16[128,128]{1,0:T(8,128)(2,1)} %get-tuple-element.7.picked) | copy-start | bytes 98308
